TPU v7x, 32 devices: a whole 2x2x4 slice. The times are simulated.
32 devices in a mesh: slab: 2 (over x), cell: 8 (over z, y), dp: 2 (over core).
Axes of the slice: x: 2, y: 2, z: 4, core: 2. Of those that a mesh axis runs over, the one named last changes fastest.
Arguments:
- sens: float32 [2, 2048, 32768], P(None, ('slab', 'dp'), 'cell'), parts along dimension 1, may hold values from -0.03125 to 0.03125
- observed: float32 [2, 2048], P(None, ('slab', 'dp')), parts along dimension 1, may hold values from -6 to 6
- noise: float32 [2, 2048], P(None, ('slab', 'dp')), parts along dimension 1, may hold values from 0.5 to 2
- survey_ids: int32 [2, 2048], P(None, ('slab', 'dp')), parts along dimension 1, may hold values from 0 to 7
- data_perturb: float32 [2, 8, 2048], P(None, None, ('slab', 'dp')), parts along dimension 2, may hold values from -6 to 6
- prior: float32 [2, 16, 32, 1024], P(None, 'slab', 'cell'), parts along dimension 1, may hold values from -6 to 6
Outputs:
- models: float32 [2, 16, 32, 1024], P(None, 'slab', 'cell'), parts along dimension 1
There are 2 independent parts, one for each index of `slab`. A program takes and returns all parts, laid end to end along the dimension named above; each array names one. Nothing has to cross between parts.
All inputs are finite; a program needn't handle non-finite values.
Results may differ from a plain program's by a relative error of at most 0.0001.
Values sent between devices are 32-bit elements; how exact they have to be, the bound alone decides.
No kernel may reach another device: no remote copies, remote signals or barrier semaphores. Data moves between devices by JAX's collectives and lax.ppermute only.
A program may use at most 64 MiB of HBM per device.

v0:
```python
import functools

import jax
import jax.numpy as jnp
from jax import lax
from jax.experimental import pallas as pl
from jax.experimental.pallas import tpu as pltpu
from jax.sharding import PartitionSpec as P

NX = 32
NSURV = 8
ITERS = 4

nu_value = 4.0
step_size = 0.5
couple_weight = 0.02
prior_weight = 0.1

LANES = 128
MIB = 2**20
BF16 = jnp.bfloat16
F32 = jnp.float32
IN_VMEM = pl.BlockSpec(memory_space=pltpu.VMEM)
IN_HBM = pl.BlockSpec(memory_space=pltpu.HBM)


def dot(left, right, along=0):
    return lax.dot_general(
        left, right, (((1,), (along,)), ((), ())), preferred_element_type=F32
    )


def resident(values):
    return pltpu.with_memory_space_constraint(values, pltpu.VMEM)


def split_rows(values):
    high = values.astype(BF16).astype(F32)
    return jnp.concatenate([high, values - high], axis=0).astype(BF16)


def fold_rows(values):
    half = values.shape[0] // 2
    return values[:half] + values[half:]


def prepare_kernel(
    block,
    sens_ref,
    prior_ref,
    ids_ref,
    split_ref,
    turned_ref,
    part_ref,
    count_ref,
    edge_ref,
    *rest,
):
    surveys, stations, _ = sens_ref.shape
    _, model_count, layers, layer_cells = prior_ref.shape
    flat_refs = rest[:surveys]
    buffers, prior_buffer, ids_buffer, semaphores, small_semaphores = rest[surveys:]
    per_survey = stations // block
    total = surveys * per_survey
    slots = buffers.shape[0]

    def copy(step):
        start = pl.multiple_of((step % per_survey) * block, block)
        slot = step % slots
        return pltpu.make_async_copy(
            sens_ref.at[step // per_survey, pl.ds(start, block), :],
            buffers.at[slot],
            semaphores.at[slot],
        )

    prior_copy = pltpu.make_async_copy(prior_ref, prior_buffer, small_semaphores.at[0])
    ids_copy = pltpu.make_async_copy(ids_ref, ids_buffer, small_semaphores.at[1])
    ahead = min(slots - 1, total)
    prior_copy.start()
    ids_copy.start()
    for step in range(min(2, ahead)):
        copy(step).start()
    prior_copy.wait()
    for step in range(min(2, ahead), ahead):
        copy(step).start()
    downward = lax.axis_index("dp") == 0
    for survey in range(surveys):
        layer_rows = [prior_buffer[survey, :, at, :] for at in range(layers)]
        for at in range(layers):
            flat_refs[survey][:, at * layer_cells : (at + 1) * layer_cells] = layer_rows[at]
        edge_ref[survey] = jnp.where(downward, layer_rows[-1], layer_rows[0])
    ids_copy.wait()
    lane = lax.broadcasted_iota(jnp.int32, (model_count, LANES), 1)
    for survey in range(surveys):
        ids = jnp.broadcast_to(ids_buffer[survey : survey + 1], (model_count, stations))
        counts = jnp.zeros((model_count, LANES), F32)
        for label in range(NSURV):
            here = jnp.sum((ids == label).astype(F32), axis=1, keepdims=True)
            counts = jnp.where(lane == NSURV + label, here, counts)
        count_ref[survey] = counts
    for survey in range(surveys):
        rows = split_rows(flat_refs[survey][...])

        def step_fn(at, carry):
            step = survey * per_survey + at
            copy(step).wait()

            @pl.when(step + slots - 1 < total)
            def _():
                copy(step + slots - 1).start()

            place = pl.ds(pl.multiple_of(at * block, block), block)
            values = buffers[step % slots]
            high = values.astype(BF16)
            low = (values - high.astype(F32)).astype(BF16)
            split_ref[0, survey, place, :] = high
            split_ref[1, survey, place, :] = low
            turned = values.T
            high_t = turned.astype(BF16)
            turned_ref[0, survey, :, place] = high_t
            turned_ref[1, survey, :, place] = (turned - high_t.astype(F32)).astype(BF16)
            part_ref[survey, :, place] = fold_rows(dot(rows, high, 1) + dot(rows, low, 1))
            return carry

        lax.fori_loop(0, per_survey, step_fn, 0)


def prepare(sens, prior, ids):
    surveys, stations, cells = sens.shape
    _, model_count, _, layer_cells = prior.shape
    block = min(stations, LANES)
    slots = 5
    outs = pl.pallas_call(
        functools.partial(prepare_kernel, block),
        out_shape=[
            pltpu.VMEM((2, surveys, stations, cells), BF16),
            pltpu.VMEM((2, surveys, cells, stations), BF16),
            jax.ShapeDtypeStruct((surveys, model_count, stations), F32),
            jax.ShapeDtypeStruct((surveys, model_count, LANES), F32),
            jax.ShapeDtypeStruct((surveys, model_count, layer_cells), F32),
        ]
        + [jax.ShapeDtypeStruct((model_count, cells), F32)] * surveys,
        in_specs=[IN_HBM] * 3,
        out_specs=[IN_VMEM] * (5 + surveys),
        scratch_shapes=[
            pltpu.VMEM((slots, block, cells), F32),
            pltpu.VMEM(prior.shape, F32),
            pltpu.VMEM(ids.shape, jnp.int32),
            pltpu.SemaphoreType.DMA((slots,)),
            pltpu.SemaphoreType.DMA((2,)),
        ],
        compiler_params=pltpu.CompilerParams(vmem_limit_bytes=12 * MIB),
        name="prepare",
    )(*[pltpu.with_memory_space_constraint(x, pltpu.HBM) for x in (sens, prior, ids)])
    return *outs[:5], list(outs[5:])


def stepped(models, prior, own, other):
    return models - step_size * ((own + other) + prior_weight * (models - prior))


def forward_kernel(survey, *refs):
    models_ref, prior_ref, own_ref, other_ref, turned_ref = refs[:5]
    models = stepped(models_ref[...], prior_ref[...], own_ref[...], other_ref[...])
    rows = split_rows(models)
    part = fold_rows(dot(rows, turned_ref[0, survey]) + dot(rows, turned_ref[1, survey]))
    refs = refs[5:]
    if survey + 1 < turned_ref.shape[1]:
        next_ref, part_ref = refs
        next_ref[...] = models
        part_ref[...] = part
        return
    earlier_models = refs[:survey]
    earlier_parts = refs[survey : 2 * survey]
    next_ref, edge_ref, part_ref = refs[2 * survey :]
    next_ref[...] = models
    part_ref[survey] = part
    for at in range(survey):
        part_ref[at] = earlier_parts[at][...]
    cells = models.shape[1]
    layer_cells = edge_ref.shape[2]
    downward = lax.axis_index("dp") == 0
    for at, ref in enumerate((*earlier_models, next_ref)):
        edge_ref[at] = jnp.where(
            downward, ref[:, cells - layer_cells :], ref[:, :layer_cells]
        )


def forward(models, prior, owns, others, turned, layer_cells):
    surveys = len(models)
    model_count, _ = models[0].shape
    stations = turned.shape[3]
    moved = []
    parts = []
    for survey in range(surveys):
        out_shape = [jax.ShapeDtypeStruct(models[survey].shape, F32)]
        operands = [models[survey], prior[survey], owns[survey], others[survey], resident(turned)]
        if survey + 1 < surveys:
            out_shape += [jax.ShapeDtypeStruct((model_count, stations), F32)]
        else:
            operands += moved + parts
            out_shape += [
                jax.ShapeDtypeStruct((surveys, model_count, layer_cells), F32),
                jax.ShapeDtypeStruct((surveys, model_count, stations), F32),
            ]
        outs = pl.pallas_call(
            functools.partial(forward_kernel, survey),
            out_shape=out_shape,
            in_specs=[IN_VMEM] * len(operands),
            out_specs=[IN_VMEM] * len(out_shape),
            compiler_params=pltpu.CompilerParams(vmem_limit_bytes=4 * MIB),
            cost_estimate=product_cost(turned),
            name="forward",
        )(*operands)
        moved.append(outs[0])
        parts.append(outs[1])
    return moved, outs[1], outs[2]


def product_cost(split):
    cells = split.shape[2] * split.shape[3]
    return pl.CostEstimate(flops=512 * cells, bytes_accessed=4 * cells, transcendentals=0)


def cross_terms(field, above, keep_x, keep_y, keep_z, depth_only):
    cells = field[0].shape[1]
    first = []
    second = []
    for grads, here, deeper in zip((first, second), field, above):
        grads.append((pltpu.roll(here, cells - 1, 1) - here) * keep_x)
        grads.append((pltpu.roll(here, cells - NX, 1) - here) * keep_y)
        change = deeper - here
        grads.append(change if keep_z is None else change * keep_z)
    cross_x = first[1] * second[2] - first[2] * second[1]
    cross_y = first[2] * second[0] - first[0] * second[2]
    cross_z = first[0] * second[1] - first[1] * second[0]
    scaling = (2.0 * couple_weight) / (
        1.0 + cross_x * cross_x + cross_y * cross_y + cross_z * cross_z
    )
    depth = [
        scaling * (second[0] * cross_y - second[1] * cross_x),
        scaling * (cross_x * first[1] - cross_y * first[0]),
    ]
    if keep_z is not None:
        depth = [value * keep_z for value in depth]
    if depth_only:
        return depth, None
    grad_x = [
        scaling * (second[1] * cross_z - second[2] * cross_y) * keep_x,
        scaling * (cross_y * first[2] - cross_z * first[1]) * keep_x,
    ]
    grad_y = [
        scaling * (second[2] * cross_x - second[0] * cross_z) * keep_y,
        scaling * (cross_z * first[0] - cross_x * first[2]) * keep_y,
    ]
    level = [
        (pltpu.roll(along_x, 1, 1) - along_x) + (pltpu.roll(along_y, NX, 1) - along_y)
        for along_x, along_y in zip(grad_x, grad_y)
    ]
    return depth, level


def couple_kernel(layer_cells, *refs):
    models_refs, edge_ref, out_refs = refs[:2], refs[2], refs[3:]
    model_count, cells = models_refs[0].shape
    layers = cells // layer_cells
    middle = layers // 2
    place = lax.broadcasted_iota(jnp.int32, (model_count, layer_cells), 1)
    keep_x = (place % NX < NX - 1).astype(F32)
    keep_y = (place < layer_cells - NX).astype(F32)
    side = lax.axis_index("dp")
    index = lax.axis_index("cell")

    def layer(at):
        if 0 <= at < layers:
            return [
                ref[:, at * layer_cells : (at + 1) * layer_cells] for ref in models_refs
            ]
        return [edge_ref[survey] for survey in range(2)]

    def write(start, stop):
        sums = {}

        def add(at, values):
            if 0 <= at < layers:
                sums[at] = values if at not in sums else [a + b for a, b in zip(sums[at], values)]

        for at in range(start, stop):
            keep_z = None
            if at < 0:
                keep_z = jnp.where(index > 0, 1.0, 0.0).astype(F32)
            elif at == layers - 1:
                keep_z = jnp.where(index < lax.axis_size("cell") - 1, 1.0, 0.0).astype(F32)
            depth, level = cross_terms(layer(at), layer(at + 1), keep_x, keep_y, keep_z, at < 0)
            if level is not None:
                add(at, [value - below for value, below in zip(level, depth)])
            add(at + 1, depth)
        for at in range(layers):
            for survey in range(2):
                spot = slice(at * layer_cells, (at + 1) * layer_cells)
                if at in sums:
                    out_refs[survey][:, spot] = sums[at][survey]
                else:
                    out_refs[survey][:, spot] = jnp.zeros((model_count, layer_cells), F32)

    @pl.when(side == 0)
    def _():
        write(middle, layers)

    @pl.when(side != 0)
    def _():
        write(-1, middle)


def couple_share(models, edge, layer_cells):
    return pl.pallas_call(
        functools.partial(couple_kernel, layer_cells),
        out_shape=[jax.ShapeDtypeStruct(x.shape, F32) for x in models],
        in_specs=[IN_VMEM] * 3,
        out_specs=[IN_VMEM] * 2,
        compiler_params=pltpu.CompilerParams(vmem_limit_bytes=4 * MIB),
        name="couple",
    )(*models, edge)


def residual_kernel(
    here_ref, there_ref, observed_ref, noise_ref, perturb_ref, ids_ref, count_ref, resid_ref, sums_ref
):
    surveys, model_count, stations = here_ref.shape
    lane = lax.broadcasted_iota(jnp.int32, (model_count, LANES), 1)
    for survey in range(surveys):
        noise = noise_ref[survey : survey + 1]
        targets = observed_ref[survey : survey + 1] + noise * perturb_ref[survey]
        resid = ((here_ref[survey] + there_ref[survey]) - targets) / noise
        resid_ref[survey] = resid
        squares = resid * resid
        ids = jnp.broadcast_to(ids_ref[survey : survey + 1], (model_count, stations))
        sums = count_ref[survey]
        for label in range(NSURV):
            here = jnp.sum(jnp.where(ids == label, squares, 0.0), axis=1, keepdims=True)
            sums = jnp.where(lane == label, here, sums)
        sums_ref[survey] = sums


def residual(here, there, observed, noise, perturb, ids, counts):
    return pl.pallas_call(
        residual_kernel,
        out_shape=[
            jax.ShapeDtypeStruct(here.shape, F32),
            jax.ShapeDtypeStruct(counts.shape, F32),
        ],
        in_specs=[IN_VMEM] * 7,
        out_specs=[IN_VMEM] * 2,
        compiler_params=pltpu.CompilerParams(vmem_limit_bytes=4 * MIB),
        name="residual",
    )(here, there, observed, noise, perturb, ids, counts)


def factor_rows(resid, sums, noise, ids):
    model_count, stations = resid.shape
    counts = pltpu.roll(sums, LANES - NSURV, 1)
    spread = (sums + 1.0) / (counts + 1.0)
    ids = jnp.broadcast_to(ids, (model_count, stations))
    spread_rows = jnp.zeros((model_count, stations), F32)
    for label in range(NSURV):
        spread_rows = jnp.where(ids == label, spread[:, label : label + 1], spread_rows)
    factor = (nu_value + 1.0) * resid / (noise * (nu_value * spread_rows + resid * resid))
    return split_rows(factor)


def spread_gradient(rows, couple_ref, split_ref, survey):
    return couple_ref[...] + fold_rows(
        dot(rows, split_ref[0, survey]) + dot(rows, split_ref[1, survey])
    )


def backward_kernel(
    resid_ref, own_ref, other_ref, noise_ref, ids_ref, couple_ref, split_ref, out_ref, *rows_refs
):
    rows = [
        factor_rows(
            resid_ref[survey],
            own_ref[survey] + other_ref[survey],
            noise_ref[survey : survey + 1],
            ids_ref[survey : survey + 1],
        )
        for survey in range(resid_ref.shape[0])
    ]
    out_ref[...] = spread_gradient(rows[0], couple_ref, split_ref, 0)
    for ref, value in zip(rows_refs, rows[1:]):
        ref[...] = value


def backward_next_kernel(survey, rows_ref, couple_ref, split_ref, out_ref):
    out_ref[...] = spread_gradient(rows_ref[...], couple_ref, split_ref, survey)


def backward(resid, own, other, noise, ids, couple, split):
    surveys, model_count, stations = resid.shape
    params = pltpu.CompilerParams(vmem_limit_bytes=4 * MIB)
    cost = product_cost(split)
    split = resident(split)
    rows_shape = jax.ShapeDtypeStruct((2 * model_count, stations), BF16)
    first, *rows = pl.pallas_call(
        backward_kernel,
        out_shape=[jax.ShapeDtypeStruct(couple[0].shape, F32)] + [rows_shape] * (surveys - 1),
        in_specs=[IN_VMEM] * 7,
        out_specs=[IN_VMEM] * surveys,
        compiler_params=params,
        cost_estimate=cost,
        name="backward",
    )(resid, own, other, noise, ids, couple[0], split)
    grads = [first]
    for survey in range(1, surveys):
        grads.append(
            pl.pallas_call(
                functools.partial(backward_next_kernel, survey),
                out_shape=jax.ShapeDtypeStruct(couple[survey].shape, F32),
                in_specs=[IN_VMEM] * 3,
                out_specs=IN_VMEM,
                compiler_params=params,
                cost_estimate=cost,
                name="backward",
            )(rows[survey - 1], couple[survey], split)
        )
    return grads


def step_kernel(models_ref, prior_ref, own_ref, other_ref, next_ref):
    next_ref[...] = stepped(models_ref[...], prior_ref[...], own_ref[...], other_ref[...])


def finish_kernel(*refs):
    out_ref = refs[-1]
    surveys, _, layers, layer_cells = out_ref.shape
    for survey in range(surveys):
        ready = survey + 1 < surveys
        models = refs[survey][...] if ready else stepped(*[ref[...] for ref in refs[survey:-1]])
        for at in range(layers):
            out_ref[survey, :, at, :] = models[:, at * layer_cells : (at + 1) * layer_cells]


def finish(models, prior, owns, others, shape):
    operands = []
    for survey in range(shape[0]):
        mine = [models[survey], prior[survey], owns[survey], others[survey]]
        if survey + 1 < shape[0]:
            mine = [
                pl.pallas_call(
                    step_kernel,
                    out_shape=jax.ShapeDtypeStruct(models[survey].shape, F32),
                    in_specs=[IN_VMEM] * 4,
                    out_specs=IN_VMEM,
                    compiler_params=pltpu.CompilerParams(vmem_limit_bytes=4 * MIB),
                    name="step",
                )(*mine)
            ]
        operands += mine
    return pl.pallas_call(
        finish_kernel,
        out_shape=jax.ShapeDtypeStruct(shape, F32),
        in_specs=[IN_VMEM] * len(operands),
        out_specs=IN_VMEM,
        compiler_params=pltpu.CompilerParams(vmem_limit_bytes=4 * MIB),
        name="finish",
    )(*operands)


def from_pair(values):
    return lax.ppermute(values, "dp", [(0, 1), (1, 0)])


def exchange_edges(edge):
    devices = lax.axis_size("cell")
    pairs = [(2 * i, 2 * i + 3) for i in range(devices - 1)]
    pairs += [(2 * i + 3, 2 * i) for i in range(devices - 1)]
    return lax.ppermute(edge, ("cell", "dp"), pairs)


def fetch(values, by, devices):
    return lax.ppermute(values, "cell", [(i, i ^ by) for i in range(devices)])


def cell_pair(values):
    devices = lax.axis_size("cell")
    stride = 1
    while devices // stride > 2:
        base = 4 if devices // stride >= 8 else 2
        total = values
        for count in range(1, base):
            total = total + fetch(values, count * stride, devices)
        values = total
        stride *= base
    return values, fetch(values, stride, devices)


def body(sens, observed, noise, ids, data_perturb, prior):
    surveys, _, _, layer_cells = prior.shape
    split, turned, part, counts, edge, flat = prepare(sens, prior, ids)
    models = flat
    for iteration in range(ITERS):
        if iteration:
            models, edge, part = forward(models, flat, owns, others, turned, layer_cells)
        edge = exchange_edges(edge)
        here, there = cell_pair(part)
        couple = couple_share(models, edge, layer_cells)
        resid, own_sums = residual(here, there, observed, noise, data_perturb, ids, counts)
        other_sums = from_pair(own_sums)
        owns = backward(resid, own_sums, other_sums, noise, ids, couple, split)
        others = [from_pair(own) for own in owns]
    return finish(models, flat, owns, others, prior.shape)


def solution(mesh):
    return jax.shard_map(
        body,
        mesh=mesh,
        in_specs=(
            P(None, ("slab", "dp"), "cell"),
            P(None, ("slab", "dp")),
            P(None, ("slab", "dp")),
            P(None, ("slab", "dp")),
            P(None, None, ("slab", "dp")),
            P(None, "slab", "cell", None),
        ),
        out_specs=P(None, "slab", "cell", None),
        check_vma=False,
    )
```

profile of v0, /device:TPU:0, one launch (start us, length us, event | category | flops | bytes accessed | tf_op | source)
XLA Modules:
  0.0 81.9 jit_solution(2995320121729145286)
XLA Ops:
  0.0 8.3 %prepare.1 = (bf16[2,2,512,4096]{3,2,1,0:T(8,128)(2,1)S(1)}, bf16[2,2,4096,512]{3,2,1,0:T(8,128)(2,1)S(1)}, f32[2,8,512]{2,1,0:T(8,128)S(1)}, f32[2,8,128]{2,1,0...) custom-call(f32[2,512,4096]{2,1,0:T(8,128)} %sens_ref.1, ...), custom_call_target="tpu_custom_call" | custom-call | tf_op jit(solution)/shard_map/prepare/pallas_call | solution.py:133
  8.3 4.1 %collective-permute-start.2 = (f32[2,8,512]{2,1,0:T(8,128)S(1)}, f32[2,8,512]{2,1,0:T(8,128)S(1)}, u32[]{:S(2)}, u32[]{:S(2)}) collective-permute-start(f32[2,8,512]{2,1,0:T(8,128)S(1)} %get-tuple-element.52), channel_id=1, source_target_pairs={{0,6},{2,4},{4,2},{6,0},{8,14},{10,12},{12,10},{14,8},{1,7},{3,5},... | collective-permute-start | bytes 98312 | tf_op jit(solution)/shard_map/ppermute | solution.py:481
  13.0 2.3 %collective-permute-start.5 = (f32[2,8,1024]{2,1,0:T(8,128)S(1)}, f32[2,8,1024]{2,1,0:T(8,128)S(1)}, u32[]{:S(2)}, u32[]{:S(2)}) collective-permute-start(f32[2,8,1024]{2,1,0:T(8,128)S(1)} %get-tuple-element.57), channel_id=1, source_target_pairs={{0,3},{2,5},{4,7},{6,9},{8,11},{10,13},{12,15},{3,0},{5,2},{7,4},{... | collective-permute-start | bytes 196616 | tf_op jit(solution)/shard_map/ppermute | solution.py:477
  16.8 2.7 %collective-permute-start.3 = (f32[2,8,512]{2,1,0:T(8,128)S(1)}, f32[2,8,512]{2,1,0:T(8,128)S(1)}, u32[]{:S(2)}, u32[]{:S(2)}) collective-permute-start(f32[2,8,512]{2,1,0:T(8,128)S(1)} %add_add_fusion.3.here_ref), channel_id=1, source_target_pairs={{0,8},{2,10},{4,12},{6,14},{8,0},{10,2},{12,4},{14,6},{1,9},{3,11}... | collective-permute-start | bytes 98312 | tf_op jit(solution)/shard_map/ppermute | solution.py:481
  19.4 2.2 %collective-permute-done.3.there_ref = f32[2,8,512]{2,1,0:T(8,128)S(1)} collective-permute-done((f32[2,8,512]{2,1,0:T(8,128)S(1)}, f32[2,8,512]{2,1,0:T(8,128)S(1)}, u32[]{:S(2)}, u32[]{:S(2)}) %collective-permute-start.3) | collective-permute-done | bytes 32800 | tf_op jit(solution)/shard_map/ppermute | solution.py:481
  23.0 1.3 %backward.8 = (f32[8,4096]{1,0:T(8,128)S(1)}, bf16[16,512]{1,0:T(8,128)(2,1)S(1)}) custom-call(f32[2,8,512]{2,1,0:T(8,128)S(1)} %get-tuple-element.54.resid_ref, f32[2,8,128]{2,1,0:T(8,128)S(1)} %get-tuple-element.55.own_ref, f32[2,8,128]{2,1,0:T(8,128)S(1)} %collective-permute-done.4.other_ref, f32[2,512]{1,0:T(2,128)S(1)} %copy-done.2, ...), custom_call_target="tpu_custom_call" | custom-call | flops 1073741824 | bytes 8388608 | tf_op jit(solution)/shard_map/backward/pallas_call | solution.py:404
  24.5 1.2 %backward.9.refs_2_ = f32[8,4096]{1,0:T(8,128)S(1)} custom-call(bf16[16,512]{1,0:T(8,128)(2,1)S(1)} %get-tuple-element.63.rows_ref, f32[8,4096]{1,0:T(8,128)S(1)} %get-tuple-element.64.couple_ref, bf16[2,2,512,4096]{3,2,1,0:T(8,128)(2,1)S(1)} %get-tuple-element.59.split_ref), custom_call_target="tpu_custom_call" | custom-call | flops 1073741824 | bytes 8388608 | tf_op jit(solution)/shard_map/backward/pallas_call | solution.py:416
  27.3 1.2 %forward.7 = (f32[8,4096]{1,0:T(8,128)S(1)}, f32[2,8,1024]{2,1,0:T(8,128)S(1)}, f32[2,8,512]{2,1,0:T(8,128)S(1)}) custom-call(f32[8,4096]{1,0:T(8,128)S(1)} %get-tuple-element.56.refs_1_.refs_0_.refs_2_, f32[8,4096]{1,0:T(8,128)S(1)} %get-tuple-element.56.refs_1_.refs_0_.refs_2_, f32[8,4096]{1,0:T(8,128)S(1)} %backward.9.refs_2_, ...), custom_call_target="tpu_custom_call" | custom-call | flops 1073741824 | bytes 8388608 | tf_op jit(solution)/shard_map/forward/pallas_call | solution.py:206
  28.5 1.5 %collective-permute-start.10 = (f32[2,8,512]{2,1,0:T(8,128)S(1)}, f32[2,8,512]{2,1,0:T(8,128)S(1)}, u32[]{:S(2)}, u32[]{:S(2)}) collective-permute-start(f32[2,8,512]{2,1,0:T(8,128)S(1)} %get-tuple-element.66), channel_id=1, source_target_pairs={{0,6},{2,4},{4,2},{6,0},{8,14},{10,12},{12,10},{14,8},{1,7},{3,5},... | collective-permute-start | bytes 98312 | tf_op jit(solution)/shard_map/ppermute | solution.py:481
  30.1 1.8 %collective-permute-start.8 = (f32[2,8,512]{2,1,0:T(8,128)S(1)}, f32[2,8,512]{2,1,0:T(8,128)S(1)}, u32[]{:S(2)}, u32[]{:S(2)}) collective-permute-start(f32[2,8,512]{2,1,0:T(8,128)S(1)} %get-tuple-element.66), channel_id=1, source_target_pairs={{0,2},{2,0},{4,6},{6,4},{8,10},{10,8},{12,14},{14,12},{1,3},{3,1},... | collective-permute-start | bytes 98312 | tf_op jit(solution)/shard_map/ppermute | solution.py:481
  32.0 1.9 %collective-permute-start.13 = (f32[2,8,1024]{2,1,0:T(8,128)S(1)}, f32[2,8,1024]{2,1,0:T(8,128)S(1)}, u32[]{:S(2)}, u32[]{:S(2)}) collective-permute-start(f32[2,8,1024]{2,1,0:T(8,128)S(1)} %get-tuple-element.70), channel_id=1, source_target_pairs={{0,3},{2,5},{4,7},{6,9},{8,11},{10,13},{12,15},{3,0},{5,2},{7,4},{... | collective-permute-start | bytes 196616 | tf_op jit(solution)/shard_map/ppermute | solution.py:477
  34.1 3.0 %collective-permute-start.11 = (f32[2,8,512]{2,1,0:T(8,128)S(1)}, f32[2,8,512]{2,1,0:T(8,128)S(1)}, u32[]{:S(2)}, u32[]{:S(2)}) collective-permute-start(f32[2,8,512]{2,1,0:T(8,128)S(1)} %add_add_fusion.2.here_ref), channel_id=1, source_target_pairs={{0,8},{2,10},{4,12},{6,14},{8,0},{10,2},{12,4},{14,6},{1,9},{3,11}... | collective-permute-start | bytes 98312 | tf_op jit(solution)/shard_map/ppermute | solution.py:481
  37.0 2.2 %collective-permute-done.11.there_ref = f32[2,8,512]{2,1,0:T(8,128)S(1)} collective-permute-done((f32[2,8,512]{2,1,0:T(8,128)S(1)}, f32[2,8,512]{2,1,0:T(8,128)S(1)}, u32[]{:S(2)}, u32[]{:S(2)}) %collective-permute-start.11) | collective-permute-done | bytes 32800 | tf_op jit(solution)/shard_map/ppermute | solution.py:481
  40.5 1.3 %backward.10 = (f32[8,4096]{1,0:T(8,128)S(1)}, bf16[16,512]{1,0:T(8,128)(2,1)S(1)}) custom-call(f32[2,8,512]{2,1,0:T(8,128)S(1)} %get-tuple-element.67.resid_ref, f32[2,8,128]{2,1,0:T(8,128)S(1)} %get-tuple-element.68.own_ref, f32[2,8,128]{2,1,0:T(8,128)S(1)} %collective-permute-done.12.other_ref, f32[2,512]{1,0:T(2,128)S(1)} %copy-done.2, ...), custom_call_target="tpu_custom_call" | custom-call | flops 1073741824 | bytes 8388608 | tf_op jit(solution)/shard_map/backward/pallas_call | solution.py:404
  42.1 1.2 %backward.11.refs_2_ = f32[8,4096]{1,0:T(8,128)S(1)} custom-call(bf16[16,512]{1,0:T(8,128)(2,1)S(1)} %get-tuple-element.74.rows_ref, f32[8,4096]{1,0:T(8,128)S(1)} %get-tuple-element.75.couple_ref, bf16[2,2,512,4096]{3,2,1,0:T(8,128)(2,1)S(1)} %get-tuple-element.59.split_ref), custom_call_target="tpu_custom_call" | custom-call | flops 1073741824 | bytes 8388608 | tf_op jit(solution)/shard_map/backward/pallas_call | solution.py:416
  43.6 1.2 %forward.8 = (f32[8,4096]{1,0:T(8,128)S(1)}, f32[8,512]{1,0:T(8,128)S(1)}) custom-call(f32[8,4096]{1,0:T(8,128)S(1)} %get-tuple-element.62.refs_5_.refs_0_, f32[8,4096]{1,0:T(8,128)S(1)} %get-tuple-element.51.refs_0_.refs_1_.prior_ref, f32[8,4096]{1,0:T(8,128)S(1)} %get-tuple-element.72.refs_2_, f32[8,4096]{1,0:T(8,128)S(1)} %collective-permute-done.14.refs_3_, ...), custom_call_target="tpu_custom_call" | custom-call | flops 1073741824 | bytes 8388608 | tf_op jit(solution)/shard_map/forward/pallas_call | solution.py:206
  44.8 1.2 %forward.9 = (f32[8,4096]{1,0:T(8,128)S(1)}, f32[2,8,1024]{2,1,0:T(8,128)S(1)}, f32[2,8,512]{2,1,0:T(8,128)S(1)}) custom-call(f32[8,4096]{1,0:T(8,128)S(1)} %get-tuple-element.69.refs_1_.refs_0_, f32[8,4096]{1,0:T(8,128)S(1)} %get-tuple-element.56.refs_1_.refs_0_.refs_2_, f32[8,4096]{1,0:T(8,128)S(1)} %backward.11.refs_2_, ...), custom_call_target="tpu_custom_call" | custom-call | flops 1073741824 | bytes 8388608 | tf_op jit(solution)/shard_map/forward/pallas_call | solution.py:206
  46.0 2.7 %collective-permute-start.18 = (f32[2,8,512]{2,1,0:T(8,128)S(1)}, f32[2,8,512]{2,1,0:T(8,128)S(1)}, u32[]{:S(2)}, u32[]{:S(2)}) collective-permute-start(f32[2,8,512]{2,1,0:T(8,128)S(1)} %get-tuple-element.77), channel_id=1, source_target_pairs={{0,6},{2,4},{4,2},{6,0},{8,14},{10,12},{12,10},{14,8},{1,7},{3,5},... | collective-permute-start | bytes 98312 | tf_op jit(solution)/shard_map/ppermute | solution.py:481
  49.5 2.4 %collective-permute-start.21 = (f32[2,8,1024]{2,1,0:T(8,128)S(1)}, f32[2,8,1024]{2,1,0:T(8,128)S(1)}, u32[]{:S(2)}, u32[]{:S(2)}) collective-permute-start(f32[2,8,1024]{2,1,0:T(8,128)S(1)} %get-tuple-element.81), channel_id=1, source_target_pairs={{0,3},{2,5},{4,7},{6,9},{8,11},{10,13},{12,15},{3,0},{5,2},{7,4},{... | collective-permute-start | bytes 196616 | tf_op jit(solution)/shard_map/ppermute | solution.py:477
  53.0 2.9 %collective-permute-start.19 = (f32[2,8,512]{2,1,0:T(8,128)S(1)}, f32[2,8,512]{2,1,0:T(8,128)S(1)}, u32[]{:S(2)}, u32[]{:S(2)}) collective-permute-start(f32[2,8,512]{2,1,0:T(8,128)S(1)} %add_add_fusion.1.here_ref), channel_id=1, source_target_pairs={{0,8},{2,10},{4,12},{6,14},{8,0},{10,2},{12,4},{14,6},{1,9},{3,11}... | collective-permute-start | bytes 98312 | tf_op jit(solution)/shard_map/ppermute | solution.py:481
  55.9 2.0 %collective-permute-done.19.there_ref = f32[2,8,512]{2,1,0:T(8,128)S(1)} collective-permute-done((f32[2,8,512]{2,1,0:T(8,128)S(1)}, f32[2,8,512]{2,1,0:T(8,128)S(1)}, u32[]{:S(2)}, u32[]{:S(2)}) %collective-permute-start.19) | collective-permute-done | bytes 32800 | tf_op jit(solution)/shard_map/ppermute | solution.py:481
  59.2 1.3 %backward.12 = (f32[8,4096]{1,0:T(8,128)S(1)}, bf16[16,512]{1,0:T(8,128)(2,1)S(1)}) custom-call(f32[2,8,512]{2,1,0:T(8,128)S(1)} %get-tuple-element.78.resid_ref, f32[2,8,128]{2,1,0:T(8,128)S(1)} %get-tuple-element.79.own_ref, f32[2,8,128]{2,1,0:T(8,128)S(1)} %collective-permute-done.20.other_ref, f32[2,512]{1,0:T(2,128)S(1)} %copy-done.2, ...), custom_call_target="tpu_custom_call" | custom-call | flops 1073741824 | bytes 8388608 | tf_op jit(solution)/shard_map/backward/pallas_call | solution.py:404
  60.7 1.2 %backward.13.refs_2_ = f32[8,4096]{1,0:T(8,128)S(1)} custom-call(bf16[16,512]{1,0:T(8,128)(2,1)S(1)} %get-tuple-element.85.rows_ref, f32[8,4096]{1,0:T(8,128)S(1)} %get-tuple-element.86.couple_ref, bf16[2,2,512,4096]{3,2,1,0:T(8,128)(2,1)S(1)} %get-tuple-element.59.split_ref), custom_call_target="tpu_custom_call" | custom-call | flops 1073741824 | bytes 8388608 | tf_op jit(solution)/shard_map/backward/pallas_call | solution.py:416
  62.3 1.2 %forward.10 = (f32[8,4096]{1,0:T(8,128)S(1)}, f32[8,512]{1,0:T(8,128)S(1)}) custom-call(f32[8,4096]{1,0:T(8,128)S(1)} %get-tuple-element.73.refs_5_.refs_0_, f32[8,4096]{1,0:T(8,128)S(1)} %get-tuple-element.51.refs_0_.refs_1_.prior_ref, f32[8,4096]{1,0:T(8,128)S(1)} %get-tuple-element.83.refs_2_, f32[8,4096]{1,0:T(8,128)S(1)} %collective-permute-done.22.refs_3_, ...), custom_call_target="tpu_custom_call" | custom-call | flops 1073741824 | bytes 8388608 | tf_op jit(solution)/shard_map/forward/pallas_call | solution.py:206
  63.5 1.2 %forward.11 = (f32[8,4096]{1,0:T(8,128)S(1)}, f32[2,8,1024]{2,1,0:T(8,128)S(1)}, f32[2,8,512]{2,1,0:T(8,128)S(1)}) custom-call(f32[8,4096]{1,0:T(8,128)S(1)} %get-tuple-element.80.refs_1_.refs_0_, f32[8,4096]{1,0:T(8,128)S(1)} %get-tuple-element.56.refs_1_.refs_0_.refs_2_, f32[8,4096]{1,0:T(8,128)S(1)} %backward.13.refs_2_, ...), custom_call_target="tpu_custom_call" | custom-call | flops 1073741824 | bytes 8388608 | tf_op jit(solution)/shard_map/forward/pallas_call | solution.py:206
  64.6 1.9 %collective-permute-start.26 = (f32[2,8,512]{2,1,0:T(8,128)S(1)}, f32[2,8,512]{2,1,0:T(8,128)S(1)}, u32[]{:S(2)}, u32[]{:S(2)}) collective-permute-start(f32[2,8,512]{2,1,0:T(8,128)S(1)} %get-tuple-element.88), channel_id=1, source_target_pairs={{0,6},{2,4},{4,2},{6,0},{8,14},{10,12},{12,10},{14,8},{1,7},{3,5},... | collective-permute-start | bytes 98312 | tf_op jit(solution)/shard_map/ppermute | solution.py:481
  66.6 1.5 %collective-permute-start.24 = (f32[2,8,512]{2,1,0:T(8,128)S(1)}, f32[2,8,512]{2,1,0:T(8,128)S(1)}, u32[]{:S(2)}, u32[]{:S(2)}) collective-permute-start(f32[2,8,512]{2,1,0:T(8,128)S(1)} %get-tuple-element.88), channel_id=1, source_target_pairs={{0,2},{2,0},{4,6},{6,4},{8,10},{10,8},{12,14},{14,12},{1,3},{3,1},... | collective-permute-start | bytes 98312 | tf_op jit(solution)/shard_map/ppermute | solution.py:481
  68.2 1.9 %collective-permute-start.29 = (f32[2,8,1024]{2,1,0:T(8,128)S(1)}, f32[2,8,1024]{2,1,0:T(8,128)S(1)}, u32[]{:S(2)}, u32[]{:S(2)}) collective-permute-start(f32[2,8,1024]{2,1,0:T(8,128)S(1)} %get-tuple-element.92), channel_id=1, source_target_pairs={{0,3},{2,5},{4,7},{6,9},{8,11},{10,13},{12,15},{3,0},{5,2},{7,4},{... | collective-permute-start | bytes 196616 | tf_op jit(solution)/shard_map/ppermute | solution.py:477
  70.6 2.9 %collective-permute-start.27 = (f32[2,8,512]{2,1,0:T(8,128)S(1)}, f32[2,8,512]{2,1,0:T(8,128)S(1)}, u32[]{:S(2)}, u32[]{:S(2)}) collective-permute-start(f32[2,8,512]{2,1,0:T(8,128)S(1)} %add_add_fusion.here_ref), channel_id=1, source_target_pairs={{0,8},{2,10},{4,12},{6,14},{8,0},{10,2},{12,4},{14,6},{1,9},{3,11}... | collective-permute-start | bytes 98312 | tf_op jit(solution)/shard_map/ppermute | solution.py:481
  73.5 2.3 %collective-permute-done.27.there_ref = f32[2,8,512]{2,1,0:T(8,128)S(1)} collective-permute-done((f32[2,8,512]{2,1,0:T(8,128)S(1)}, f32[2,8,512]{2,1,0:T(8,128)S(1)}, u32[]{:S(2)}, u32[]{:S(2)}) %collective-permute-start.27) | collective-permute-done | bytes 32800 | tf_op jit(solution)/shard_map/ppermute | solution.py:481
  77.1 1.3 %backward.14 = (f32[8,4096]{1,0:T(8,128)S(1)}, bf16[16,512]{1,0:T(8,128)(2,1)S(1)}) custom-call(f32[2,8,512]{2,1,0:T(8,128)S(1)} %get-tuple-element.89.resid_ref, f32[2,8,128]{2,1,0:T(8,128)S(1)} %get-tuple-element.90.own_ref, f32[2,8,128]{2,1,0:T(8,128)S(1)} %collective-permute-done.28.other_ref, f32[2,512]{1,0:T(2,128)S(1)} %copy-done.2, ...), custom_call_target="tpu_custom_call" | custom-call | flops 1073741824 | bytes 8388608 | tf_op jit(solution)/shard_map/backward/pallas_call | solution.py:404
  78.6 1.2 %backward.15.refs_3_ = f32[8,4096]{1,0:T(8,128)S(1)} custom-call(bf16[16,512]{1,0:T(8,128)(2,1)S(1)} %get-tuple-element.95.rows_ref, f32[8,4096]{1,0:T(8,128)S(1)} %get-tuple-element.96.couple_ref, bf16[2,2,512,4096]{3,2,1,0:T(8,128)(2,1)S(1)} %get-tuple-element.59.split_ref), custom_call_target="tpu_custom_call" | custom-call | flops 1073741824 | bytes 8388608 | tf_op jit(solution)/shard_map/backward/pallas_call | solution.py:416
  (69 shorter events, 15.2 us)
Async XLA Ops:
  8.3 7.0 %collective-permute-start.2 = (f32[2,8,512]{2,1,0:T(8,128)S(1)}, f32[2,8,512]{2,1,0:T(8,128)S(1)}, u32[]{:S(2)}, u32[]{:S(2)}) collective-permute-start(f32[2,8,512]{2,1,0:T(8,128)S(1)} %get-tuple-element.52), channel_id=1, source_target_pairs={{0,6},{2,4},{4,2},{6,0},{8,14},{10,12},{12,10},{14,8},{1,7},{3,5},... | collective-permute-start | bytes 98312 | tf_op jit(solution)/shard_map/ppermute | solution.py:481
  12.4 3.9 %collective-permute-start.1 = (f32[2,8,512]{2,1,0:T(8,128)S(1)}, f32[2,8,512]{2,1,0:T(8,128)S(1)}, u32[]{:S(2)}, u32[]{:S(2)}) collective-permute-start(f32[2,8,512]{2,1,0:T(8,128)S(1)} %get-tuple-element.52), channel_id=1, source_target_pairs={{0,4},{2,6},{4,0},{6,2},{8,12},{10,14},{12,8},{14,10},{1,5},{3,7},... | collective-permute-start | bytes 98312 | tf_op jit(solution)/shard_map/ppermute | solution.py:481
  12.8 3.9 %collective-permute-start = (f32[2,8,512]{2,1,0:T(8,128)S(1)}, f32[2,8,512]{2,1,0:T(8,128)S(1)}, u32[]{:S(2)}, u32[]{:S(2)}) collective-permute-start(f32[2,8,512]{2,1,0:T(8,128)S(1)} %get-tuple-element.52), channel_id=1, source_target_pairs={{0,2},{2,0},{4,6},{6,4},{8,10},{10,8},{12,14},{14,12},{1,3},{3,1},... | collective-permute-start | bytes 98312 | tf_op jit(solution)/shard_map/ppermute | solution.py:481
  13.0 8.8 %collective-permute-start.5 = (f32[2,8,1024]{2,1,0:T(8,128)S(1)}, f32[2,8,1024]{2,1,0:T(8,128)S(1)}, u32[]{:S(2)}, u32[]{:S(2)}) collective-permute-start(f32[2,8,1024]{2,1,0:T(8,128)S(1)} %get-tuple-element.57), channel_id=1, source_target_pairs={{0,3},{2,5},{4,7},{6,9},{8,11},{10,13},{12,15},{3,0},{5,2},{7,4},{... | collective-permute-start | bytes 196616 | tf_op jit(solution)/shard_map/ppermute | solution.py:477
  16.8 4.9 %collective-permute-start.3 = (f32[2,8,512]{2,1,0:T(8,128)S(1)}, f32[2,8,512]{2,1,0:T(8,128)S(1)}, u32[]{:S(2)}, u32[]{:S(2)}) collective-permute-start(f32[2,8,512]{2,1,0:T(8,128)S(1)} %add_add_fusion.3.here_ref), channel_id=1, source_target_pairs={{0,8},{2,10},{4,12},{6,14},{8,0},{10,2},{12,4},{14,6},{1,9},{3,11}... | collective-permute-start | bytes 98312 | tf_op jit(solution)/shard_map/ppermute | solution.py:481
  21.8 1.2 %collective-permute-start.4 = (f32[2,8,128]{2,1,0:T(8,128)S(1)}, f32[2,8,128]{2,1,0:T(8,128)S(1)}, u32[]{:S(2)}, u32[]{:S(2)}) collective-permute-start(f32[2,8,128]{2,1,0:T(8,128)S(1)} %get-tuple-element.55.own_ref), channel_id=1, source_target_pairs={{0,1},{1,0},{2,3},{3,2},{4,5},{5,4},{6,7},{7,6},{8,9},{9,8},{10,11... | collective-permute-start | bytes 24584 | tf_op jit(solution)/shard_map/ppermute | solution.py:470
  24.3 1.7 %collective-permute-start.6 = (f32[8,4096]{1,0:T(8,128)S(1)}, f32[8,4096]{1,0:T(8,128)S(1)}, u32[]{:S(2)}, u32[]{:S(2)}) collective-permute-start(f32[8,4096]{1,0:T(8,128)S(1)} %get-tuple-element.60.refs_2_), channel_id=1, source_target_pairs={{0,1},{1,0},{2,3},{3,2},{4,5},{5,4},{6,7},{7,6},{8,9},{9,8},{10,11... | collective-permute-start | bytes 393224 | tf_op jit(solution)/shard_map/ppermute | solution.py:470
  25.7 1.5 %collective-permute-start.7 = (f32[8,4096]{1,0:T(8,128)S(1)}, f32[8,4096]{1,0:T(8,128)S(1)}, u32[]{:S(2)}, u32[]{:S(2)}) collective-permute-start(f32[8,4096]{1,0:T(8,128)S(1)} %backward.9.refs_2_), channel_id=1, source_target_pairs={{0,1},{1,0},{2,3},{3,2},{4,5},{5,4},{6,7},{7,6},{8,9},{9,8},{10,11... | collective-permute-start | bytes 393224 | tf_op jit(solution)/shard_map/ppermute | solution.py:470
  28.5 5.4 %collective-permute-start.10 = (f32[2,8,512]{2,1,0:T(8,128)S(1)}, f32[2,8,512]{2,1,0:T(8,128)S(1)}, u32[]{:S(2)}, u32[]{:S(2)}) collective-permute-start(f32[2,8,512]{2,1,0:T(8,128)S(1)} %get-tuple-element.66), channel_id=1, source_target_pairs={{0,6},{2,4},{4,2},{6,0},{8,14},{10,12},{12,10},{14,8},{1,7},{3,5},... | collective-permute-start | bytes 98312 | tf_op jit(solution)/shard_map/ppermute | solution.py:481
  30.0 3.9 %collective-permute-start.9 = (f32[2,8,512]{2,1,0:T(8,128)S(1)}, f32[2,8,512]{2,1,0:T(8,128)S(1)}, u32[]{:S(2)}, u32[]{:S(2)}) collective-permute-start(f32[2,8,512]{2,1,0:T(8,128)S(1)} %get-tuple-element.66), channel_id=1, source_target_pairs={{0,4},{2,6},{4,0},{6,2},{8,12},{10,14},{12,8},{14,10},{1,5},{3,7},... | collective-permute-start | bytes 98312 | tf_op jit(solution)/shard_map/ppermute | solution.py:481
  30.1 3.9 %collective-permute-start.8 = (f32[2,8,512]{2,1,0:T(8,128)S(1)}, f32[2,8,512]{2,1,0:T(8,128)S(1)}, u32[]{:S(2)}, u32[]{:S(2)}) collective-permute-start(f32[2,8,512]{2,1,0:T(8,128)S(1)} %get-tuple-element.66), channel_id=1, source_target_pairs={{0,2},{2,0},{4,6},{6,4},{8,10},{10,8},{12,14},{14,12},{1,3},{3,1},... | collective-permute-start | bytes 98312 | tf_op jit(solution)/shard_map/ppermute | solution.py:481
  32.0 7.5 %collective-permute-start.13 = (f32[2,8,1024]{2,1,0:T(8,128)S(1)}, f32[2,8,1024]{2,1,0:T(8,128)S(1)}, u32[]{:S(2)}, u32[]{:S(2)}) collective-permute-start(f32[2,8,1024]{2,1,0:T(8,128)S(1)} %get-tuple-element.70), channel_id=1, source_target_pairs={{0,3},{2,5},{4,7},{6,9},{8,11},{10,13},{12,15},{3,0},{5,2},{7,4},{... | collective-permute-start | bytes 196616 | tf_op jit(solution)/shard_map/ppermute | solution.py:477
  34.1 5.1 %collective-permute-start.11 = (f32[2,8,512]{2,1,0:T(8,128)S(1)}, f32[2,8,512]{2,1,0:T(8,128)S(1)}, u32[]{:S(2)}, u32[]{:S(2)}) collective-permute-start(f32[2,8,512]{2,1,0:T(8,128)S(1)} %add_add_fusion.2.here_ref), channel_id=1, source_target_pairs={{0,8},{2,10},{4,12},{6,14},{8,0},{10,2},{12,4},{14,6},{1,9},{3,11}... | collective-permute-start | bytes 98312 | tf_op jit(solution)/shard_map/ppermute | solution.py:481
  39.3 1.2 %collective-permute-start.12 = (f32[2,8,128]{2,1,0:T(8,128)S(1)}, f32[2,8,128]{2,1,0:T(8,128)S(1)}, u32[]{:S(2)}, u32[]{:S(2)}) collective-permute-start(f32[2,8,128]{2,1,0:T(8,128)S(1)} %get-tuple-element.68.own_ref), channel_id=1, source_target_pairs={{0,1},{1,0},{2,3},{3,2},{4,5},{5,4},{6,7},{7,6},{8,9},{9,8},{10,11... | collective-permute-start | bytes 24584 | tf_op jit(solution)/shard_map/ppermute | solution.py:470
  41.9 1.7 %collective-permute-start.14 = (f32[8,4096]{1,0:T(8,128)S(1)}, f32[8,4096]{1,0:T(8,128)S(1)}, u32[]{:S(2)}, u32[]{:S(2)}) collective-permute-start(f32[8,4096]{1,0:T(8,128)S(1)} %get-tuple-element.72.refs_2_), channel_id=1, source_target_pairs={{0,1},{1,0},{2,3},{3,2},{4,5},{5,4},{6,7},{7,6},{8,9},{9,8},{10,11... | collective-permute-start | bytes 393224 | tf_op jit(solution)/shard_map/ppermute | solution.py:470
  43.2 1.5 %collective-permute-start.15 = (f32[8,4096]{1,0:T(8,128)S(1)}, f32[8,4096]{1,0:T(8,128)S(1)}, u32[]{:S(2)}, u32[]{:S(2)}) collective-permute-start(f32[8,4096]{1,0:T(8,128)S(1)} %backward.11.refs_2_), channel_id=1, source_target_pairs={{0,1},{1,0},{2,3},{3,2},{4,5},{5,4},{6,7},{7,6},{8,9},{9,8},{10,11... | collective-permute-start | bytes 393224 | tf_op jit(solution)/shard_map/ppermute | solution.py:470
  46.0 5.9 %collective-permute-start.18 = (f32[2,8,512]{2,1,0:T(8,128)S(1)}, f32[2,8,512]{2,1,0:T(8,128)S(1)}, u32[]{:S(2)}, u32[]{:S(2)}) collective-permute-start(f32[2,8,512]{2,1,0:T(8,128)S(1)} %get-tuple-element.77), channel_id=1, source_target_pairs={{0,6},{2,4},{4,2},{6,0},{8,14},{10,12},{12,10},{14,8},{1,7},{3,5},... | collective-permute-start | bytes 98312 | tf_op jit(solution)/shard_map/ppermute | solution.py:481
  48.7 3.9 %collective-permute-start.17 = (f32[2,8,512]{2,1,0:T(8,128)S(1)}, f32[2,8,512]{2,1,0:T(8,128)S(1)}, u32[]{:S(2)}, u32[]{:S(2)}) collective-permute-start(f32[2,8,512]{2,1,0:T(8,128)S(1)} %get-tuple-element.77), channel_id=1, source_target_pairs={{0,4},{2,6},{4,0},{6,2},{8,12},{10,14},{12,8},{14,10},{1,5},{3,7},... | collective-permute-start | bytes 98312 | tf_op jit(solution)/shard_map/ppermute | solution.py:481
  49.0 3.9 %collective-permute-start.16 = (f32[2,8,512]{2,1,0:T(8,128)S(1)}, f32[2,8,512]{2,1,0:T(8,128)S(1)}, u32[]{:S(2)}, u32[]{:S(2)}) collective-permute-start(f32[2,8,512]{2,1,0:T(8,128)S(1)} %get-tuple-element.77), channel_id=1, source_target_pairs={{0,2},{2,0},{4,6},{6,4},{8,10},{10,8},{12,14},{14,12},{1,3},{3,1},... | collective-permute-start | bytes 98312 | tf_op jit(solution)/shard_map/ppermute | solution.py:481
  49.5 8.6 %collective-permute-start.21 = (f32[2,8,1024]{2,1,0:T(8,128)S(1)}, f32[2,8,1024]{2,1,0:T(8,128)S(1)}, u32[]{:S(2)}, u32[]{:S(2)}) collective-permute-start(f32[2,8,1024]{2,1,0:T(8,128)S(1)} %get-tuple-element.81), channel_id=1, source_target_pairs={{0,3},{2,5},{4,7},{6,9},{8,11},{10,13},{12,15},{3,0},{5,2},{7,4},{... | collective-permute-start | bytes 196616 | tf_op jit(solution)/shard_map/ppermute | solution.py:477
  53.0 4.9 %collective-permute-start.19 = (f32[2,8,512]{2,1,0:T(8,128)S(1)}, f32[2,8,512]{2,1,0:T(8,128)S(1)}, u32[]{:S(2)}, u32[]{:S(2)}) collective-permute-start(f32[2,8,512]{2,1,0:T(8,128)S(1)} %add_add_fusion.1.here_ref), channel_id=1, source_target_pairs={{0,8},{2,10},{4,12},{6,14},{8,0},{10,2},{12,4},{14,6},{1,9},{3,11}... | collective-permute-start | bytes 98312 | tf_op jit(solution)/shard_map/ppermute | solution.py:481
  58.0 1.2 %collective-permute-start.20 = (f32[2,8,128]{2,1,0:T(8,128)S(1)}, f32[2,8,128]{2,1,0:T(8,128)S(1)}, u32[]{:S(2)}, u32[]{:S(2)}) collective-permute-start(f32[2,8,128]{2,1,0:T(8,128)S(1)} %get-tuple-element.79.own_ref), channel_id=1, source_target_pairs={{0,1},{1,0},{2,3},{3,2},{4,5},{5,4},{6,7},{7,6},{8,9},{9,8},{10,11... | collective-permute-start | bytes 24584 | tf_op jit(solution)/shard_map/ppermute | solution.py:470
  60.5 1.7 %collective-permute-start.22 = (f32[8,4096]{1,0:T(8,128)S(1)}, f32[8,4096]{1,0:T(8,128)S(1)}, u32[]{:S(2)}, u32[]{:S(2)}) collective-permute-start(f32[8,4096]{1,0:T(8,128)S(1)} %get-tuple-element.83.refs_2_), channel_id=1, source_target_pairs={{0,1},{1,0},{2,3},{3,2},{4,5},{5,4},{6,7},{7,6},{8,9},{9,8},{10,11... | collective-permute-start | bytes 393224 | tf_op jit(solution)/shard_map/ppermute | solution.py:470
  61.9 1.5 %collective-permute-start.23 = (f32[8,4096]{1,0:T(8,128)S(1)}, f32[8,4096]{1,0:T(8,128)S(1)}, u32[]{:S(2)}, u32[]{:S(2)}) collective-permute-start(f32[8,4096]{1,0:T(8,128)S(1)} %backward.13.refs_2_), channel_id=1, source_target_pairs={{0,1},{1,0},{2,3},{3,2},{4,5},{5,4},{6,7},{7,6},{8,9},{9,8},{10,11... | collective-permute-start | bytes 393224 | tf_op jit(solution)/shard_map/ppermute | solution.py:470
  64.6 5.4 %collective-permute-start.26 = (f32[2,8,512]{2,1,0:T(8,128)S(1)}, f32[2,8,512]{2,1,0:T(8,128)S(1)}, u32[]{:S(2)}, u32[]{:S(2)}) collective-permute-start(f32[2,8,512]{2,1,0:T(8,128)S(1)} %get-tuple-element.88), channel_id=1, source_target_pairs={{0,6},{2,4},{4,2},{6,0},{8,14},{10,12},{12,10},{14,8},{1,7},{3,5},... | collective-permute-start | bytes 98312 | tf_op jit(solution)/shard_map/ppermute | solution.py:481
  66.6 3.9 %collective-permute-start.25 = (f32[2,8,512]{2,1,0:T(8,128)S(1)}, f32[2,8,512]{2,1,0:T(8,128)S(1)}, u32[]{:S(2)}, u32[]{:S(2)}) collective-permute-start(f32[2,8,512]{2,1,0:T(8,128)S(1)} %get-tuple-element.88), channel_id=1, source_target_pairs={{0,4},{2,6},{4,0},{6,2},{8,12},{10,14},{12,8},{14,10},{1,5},{3,7},... | collective-permute-start | bytes 98312 | tf_op jit(solution)/shard_map/ppermute | solution.py:481
  66.6 3.9 %collective-permute-start.24 = (f32[2,8,512]{2,1,0:T(8,128)S(1)}, f32[2,8,512]{2,1,0:T(8,128)S(1)}, u32[]{:S(2)}, u32[]{:S(2)}) collective-permute-start(f32[2,8,512]{2,1,0:T(8,128)S(1)} %get-tuple-element.88), channel_id=1, source_target_pairs={{0,2},{2,0},{4,6},{6,4},{8,10},{10,8},{12,14},{14,12},{1,3},{3,1},... | collective-permute-start | bytes 98312 | tf_op jit(solution)/shard_map/ppermute | solution.py:481
  68.2 7.9 %collective-permute-start.29 = (f32[2,8,1024]{2,1,0:T(8,128)S(1)}, f32[2,8,1024]{2,1,0:T(8,128)S(1)}, u32[]{:S(2)}, u32[]{:S(2)}) collective-permute-start(f32[2,8,1024]{2,1,0:T(8,128)S(1)} %get-tuple-element.92), channel_id=1, source_target_pairs={{0,3},{2,5},{4,7},{6,9},{8,11},{10,13},{12,15},{3,0},{5,2},{7,4},{... | collective-permute-start | bytes 196616 | tf_op jit(solution)/shard_map/ppermute | solution.py:477
  70.6 5.2 %collective-permute-start.27 = (f32[2,8,512]{2,1,0:T(8,128)S(1)}, f32[2,8,512]{2,1,0:T(8,128)S(1)}, u32[]{:S(2)}, u32[]{:S(2)}) collective-permute-start(f32[2,8,512]{2,1,0:T(8,128)S(1)} %add_add_fusion.here_ref), channel_id=1, source_target_pairs={{0,8},{2,10},{4,12},{6,14},{8,0},{10,2},{12,4},{14,6},{1,9},{3,11}... | collective-permute-start | bytes 98312 | tf_op jit(solution)/shard_map/ppermute | solution.py:481
  75.9 1.2 %collective-permute-start.28 = (f32[2,8,128]{2,1,0:T(8,128)S(1)}, f32[2,8,128]{2,1,0:T(8,128)S(1)}, u32[]{:S(2)}, u32[]{:S(2)}) collective-permute-start(f32[2,8,128]{2,1,0:T(8,128)S(1)} %get-tuple-element.90.own_ref), channel_id=1, source_target_pairs={{0,1},{1,0},{2,3},{3,2},{4,5},{5,4},{6,7},{7,6},{8,9},{9,8},{10,11... | collective-permute-start | bytes 24584 | tf_op jit(solution)/shard_map/ppermute | solution.py:470
  78.4 1.7 %collective-permute-start.30 = (f32[8,4096]{1,0:T(8,128)S(1)}, f32[8,4096]{1,0:T(8,128)S(1)}, u32[]{:S(2)}, u32[]{:S(2)}) collective-permute-start(f32[8,4096]{1,0:T(8,128)S(1)} %get-tuple-element.94.own_ref), channel_id=1, source_target_pairs={{0,1},{1,0},{2,3},{3,2},{4,5},{5,4},{6,7},{7,6},{8,9},{9,8},{10,11... | collective-permute-start | bytes 393224 | tf_op jit(solution)/shard_map/ppermute | solution.py:470
  79.8 1.4 %collective-permute-start.31 = (f32[8,4096]{1,0:T(8,128)S(1)}, f32[8,4096]{1,0:T(8,128)S(1)}, u32[]{:S(2)}, u32[]{:S(2)}) collective-permute-start(f32[8,4096]{1,0:T(8,128)S(1)} %backward.15.refs_3_), channel_id=1, source_target_pairs={{0,1},{1,0},{2,3},{3,2},{4,5},{5,4},{6,7},{7,6},{8,9},{9,8},{10,11... | collective-permute-start | bytes 393224 | tf_op jit(solution)/shard_map/ppermute | solution.py:470
  (4 other events, 86.6 us)
where the time goes:
time: 82.2 us; the launch traced here: 81.9 us
  starting transfers between devices  37.8 us (46%)
  Pallas kernels  28.1 us (34%)
  waiting for transfers between devices  15.7 us (19%)
    ppermute x16, starting transfers between devices, fetch(): return lax.ppermute(values, 'cell', [(i, i ^ by) for i in range(devices)])  26.7 us
    ppermute x16, waiting for transfers between devices, fetch(): return lax.ppermute(values, 'cell', [(i, i ^ by) for i in range(devices)])  11.7 us
    ppermute x4, starting transfers between devices, exchange_edges(): return lax.ppermute(edge, ('cell', 'dp'), pairs)  8.55 us
    pallas_call x1, Pallas kernels, prepare(): pl.pallas_call(functools.partial(prepare_kernel, block), out_shape=[pltpu...  8.31 us
    pallas_call x6, Pallas kernels, forward(): pl.pallas_call(functools.partial(forward_kernel, survey), out_shape=out_s...  7.13 us
    pallas_call x4, Pallas kernels, backward(): pl.pallas_call(backward_kernel, out_shape=[jax.ShapeDtypeStruct(couple[0]...  5.32 us
    pallas_call x4, Pallas kernels, backward(): pl.pallas_call(functools.partial(backward_next_kernel, survey), out_shape...  4.74 us
    ppermute x12, waiting for transfers between devices, from_pair(): return lax.ppermute(values, 'dp', [(0, 1), (1, 0)])  4.06 us
  transfers between devices with their start and end apart: 32, of which 16 were waited for; matrix products, arithmetic and copies ran while one was open for 0% of the time, Pallas kernels for 12%

commit v1 on v0

--- a/solution.py
+++ b/solution.py
@@ -391,11 +391,15 @@
         ref[...] = value
 
 
-def backward_next_kernel(survey, rows_ref, couple_ref, split_ref, out_ref):
-    out_ref[...] = spread_gradient(rows_ref[...], couple_ref, split_ref, survey)
-
-
-def backward(resid, own, other, noise, ids, couple, split):
+def backward_next_kernel(survey, start, rows_ref, couple_ref, split_ref, out_ref):
+    spot = slice(start, start + out_ref.shape[1])
+    rows = rows_ref[...]
+    out_ref[...] = couple_ref[:, spot] + fold_rows(
+        dot(rows, split_ref[0, survey, :, spot]) + dot(rows, split_ref[1, survey, :, spot])
+    )
+
+
+def backward(resid, own, other, noise, ids, couple, split, pieces):
     surveys, model_count, stations = resid.shape
     params = pltpu.CompilerParams(vmem_limit_bytes=4 * MIB)
     cost = product_cost(split)
@@ -411,11 +415,12 @@
         name="backward",
     )(resid, own, other, noise, ids, couple[0], split)
     grads = [first]
-    for survey in range(1, surveys):
+    for survey, at in [(s, p) for s in range(1, surveys) for p in range(pieces)]:
+        width = couple[survey].shape[1] // pieces
         grads.append(
             pl.pallas_call(
-                functools.partial(backward_next_kernel, survey),
-                out_shape=jax.ShapeDtypeStruct(couple[survey].shape, F32),
+                functools.partial(backward_next_kernel, survey, at * width),
+                out_shape=jax.ShapeDtypeStruct((model_count, width), F32),
                 in_specs=[IN_VMEM] * 3,
                 out_specs=IN_VMEM,
                 compiler_params=params,
@@ -435,7 +440,13 @@
     surveys, _, layers, layer_cells = out_ref.shape
     for survey in range(surveys):
         ready = survey + 1 < surveys
-        models = refs[survey][...] if ready else stepped(*[ref[...] for ref in refs[survey:-1]])
+        if ready:
+            models = refs[survey][...]
+        else:
+            tail = [ref[...] for ref in refs[survey + 2 : -1]]
+            half = len(tail) // 2
+            sides = [jnp.concatenate(x, axis=1) for x in (tail[:half], tail[half:])]
+            models = stepped(refs[survey][...], refs[survey + 1][...], *sides)
         for at in range(layers):
             out_ref[survey, :, at, :] = models[:, at * layer_cells : (at + 1) * layer_cells]
 
@@ -443,8 +454,11 @@
 def finish(models, prior, owns, others, shape):
     operands = []
     for survey in range(shape[0]):
-        mine = [models[survey], prior[survey], owns[survey], others[survey]]
-        if survey + 1 < shape[0]:
+        mine = [models[survey], prior[survey]]
+        if survey + 1 == shape[0]:
+            mine += [*owns[survey:], *others[survey:]]
+        else:
+            mine += [owns[survey], others[survey]]
             mine = [
                 pl.pallas_call(
                     step_kernel,
@@ -506,7 +520,7 @@
         couple = couple_share(models, edge, layer_cells)
         resid, own_sums = residual(here, there, observed, noise, data_perturb, ids, counts)
         other_sums = from_pair(own_sums)
-        owns = backward(resid, own_sums, other_sums, noise, ids, couple, split)
+        owns = backward(resid, own_sums, other_sums, noise, ids, couple, split, 1 if iteration + 1 < ITERS else 2)
         others = [from_pair(own) for own in owns]
     return finish(models, flat, owns, others, prior.shape)
 

time: 82.2 us -> 82.5 us (level)
    ppermute x12 -> x13, starting transfers between devices: 2.61 us -> 2.77 us  [from_pair(): return lax.ppermute(values, 'dp', [(0, 1), (1, 0)])]
    pallas_call x4 -> x5, Pallas kernels: 4.74 us -> 4.86 us  [backward(): pl.pallas_call(functools.partial(backward_next_kernel, survey, at * width...]
    ppermute x12 -> x13, waiting for transfers between devices: 4.06 us -> 4.14 us  [from_pair(): return lax.ppermute(values, 'dp', [(0, 1), (1, 0)])]
  transfers between devices with their start and end apart: 32 -> 33, of which waited for: 16 -> 17; matrix products, arithmetic and copies ran while one was open for 0% -> 0% of each run, Pallas kernels for 12% -> 12%
where the time goes in v1:
time: 82.5 us; the launch traced here: 82.3 us
  starting transfers between devices  38 us (46%)
  Pallas kernels  28.2 us (34%)
  waiting for transfers between devices  15.8 us (19%)
    ppermute x16, starting transfers between devices, fetch(): return lax.ppermute(values, 'cell', [(i, i ^ by) for i in range(devices)])  26.7 us
    ppermute x16, waiting for transfers between devices, fetch(): return lax.ppermute(values, 'cell', [(i, i ^ by) for i in range(devices)])  11.7 us
    ppermute x4, starting transfers between devices, exchange_edges(): return lax.ppermute(edge, ('cell', 'dp'), pairs)  8.55 us
    pallas_call x1, Pallas kernels, prepare(): pl.pallas_call(functools.partial(prepare_kernel, block), out_shape=[pltpu...  8.31 us
    pallas_call x6, Pallas kernels, forward(): pl.pallas_call(functools.partial(forward_kernel, survey), out_shape=out_s...  7.13 us
    pallas_call x4, Pallas kernels, backward(): pl.pallas_call(backward_kernel, out_shape=[jax.ShapeDtypeStruct(couple[0]...  5.32 us
    pallas_call x5, Pallas kernels, backward(): pl.pallas_call(functools.partial(backward_next_kernel, survey, at * width...  4.86 us
    ppermute x13, waiting for transfers between devices, from_pair(): return lax.ppermute(values, 'dp', [(0, 1), (1, 0)])  4.14 us
  transfers between devices with their start and end apart: 33, of which 17 were waited for; matrix products, arithmetic and copies ran while one was open for 0% of the time, Pallas kernels for 12%

profile of v1, /device:TPU:0, one launch (start us, length us, event | category | flops | bytes accessed | tf_op | source)
XLA Modules:
  0.0 82.3 jit_solution(14198922130817939478)
XLA Ops:
  0.0 8.3 %prepare.1 = (bf16[2,2,512,4096]{3,2,1,0:T(8,128)(2,1)S(1)}, bf16[2,2,4096,512]{3,2,1,0:T(8,128)(2,1)S(1)}, f32[2,8,512]{2,1,0:T(8,128)S(1)}, f32[2,8,128]{2,1,0...) custom-call(f32[2,512,4096]{2,1,0:T(8,128)} %sens_ref.1, ...), custom_call_target="tpu_custom_call" | custom-call | tf_op jit(solution)/shard_map/prepare/pallas_call | solution.py:133
  8.3 4.1 %collective-permute-start.2 = (f32[2,8,512]{2,1,0:T(8,128)S(1)}, f32[2,8,512]{2,1,0:T(8,128)S(1)}, u32[]{:S(2)}, u32[]{:S(2)}) collective-permute-start(f32[2,8,512]{2,1,0:T(8,128)S(1)} %get-tuple-element.52), channel_id=1, source_target_pairs={{0,6},{2,4},{4,2},{6,0},{8,14},{10,12},{12,10},{14,8},{1,7},{3,5},... | collective-permute-start | bytes 98312 | tf_op jit(solution)/shard_map/ppermute | solution.py:495
  13.0 2.3 %collective-permute-start.5 = (f32[2,8,1024]{2,1,0:T(8,128)S(1)}, f32[2,8,1024]{2,1,0:T(8,128)S(1)}, u32[]{:S(2)}, u32[]{:S(2)}) collective-permute-start(f32[2,8,1024]{2,1,0:T(8,128)S(1)} %get-tuple-element.57), channel_id=1, source_target_pairs={{0,3},{2,5},{4,7},{6,9},{8,11},{10,13},{12,15},{3,0},{5,2},{7,4},{... | collective-permute-start | bytes 196616 | tf_op jit(solution)/shard_map/ppermute | solution.py:491
  16.8 2.7 %collective-permute-start.3 = (f32[2,8,512]{2,1,0:T(8,128)S(1)}, f32[2,8,512]{2,1,0:T(8,128)S(1)}, u32[]{:S(2)}, u32[]{:S(2)}) collective-permute-start(f32[2,8,512]{2,1,0:T(8,128)S(1)} %add_add_fusion.3.here_ref), channel_id=1, source_target_pairs={{0,8},{2,10},{4,12},{6,14},{8,0},{10,2},{12,4},{14,6},{1,9},{3,11}... | collective-permute-start | bytes 98312 | tf_op jit(solution)/shard_map/ppermute | solution.py:495
  19.4 2.2 %collective-permute-done.3.there_ref = f32[2,8,512]{2,1,0:T(8,128)S(1)} collective-permute-done((f32[2,8,512]{2,1,0:T(8,128)S(1)}, f32[2,8,512]{2,1,0:T(8,128)S(1)}, u32[]{:S(2)}, u32[]{:S(2)}) %collective-permute-start.3) | collective-permute-done | bytes 32800 | tf_op jit(solution)/shard_map/ppermute | solution.py:495
  23.0 1.3 %backward.9 = (f32[8,4096]{1,0:T(8,128)S(1)}, bf16[16,512]{1,0:T(8,128)(2,1)S(1)}) custom-call(f32[2,8,512]{2,1,0:T(8,128)S(1)} %get-tuple-element.54.resid_ref, f32[2,8,128]{2,1,0:T(8,128)S(1)} %get-tuple-element.55.own_ref, f32[2,8,128]{2,1,0:T(8,128)S(1)} %collective-permute-done.4.other_ref, f32[2,512]{1,0:T(2,128)S(1)} %copy-done.2, ...), custom_call_target="tpu_custom_call" | custom-call | flops 1073741824 | bytes 8388608 | tf_op jit(solution)/shard_map/backward/pallas_call | solution.py:408
  24.5 1.2 %backward.10.refs_2_ = f32[8,4096]{1,0:T(8,128)S(1)} custom-call(bf16[16,512]{1,0:T(8,128)(2,1)S(1)} %get-tuple-element.63.rows_ref, f32[8,4096]{1,0:T(8,128)S(1)} %get-tuple-element.64.couple_ref, bf16[2,2,512,4096]{3,2,1,0:T(8,128)(2,1)S(1)} %get-tuple-element.59.split_ref), custom_call_target="tpu_custom_call" | custom-call | flops 1073741824 | bytes 8388608 | tf_op jit(solution)/shard_map/backward/pallas_call | solution.py:421
  26.1 1.2 %forward.6 = (f32[8,4096]{1,0:T(8,128)S(1)}, f32[8,512]{1,0:T(8,128)S(1)}) custom-call(f32[8,4096]{1,0:T(8,128)S(1)} %get-tuple-element.51.refs_0_.refs_1_.prior_ref, f32[8,4096]{1,0:T(8,128)S(1)} %get-tuple-element.51.refs_0_.refs_1_.prior_ref, f32[8,4096]{1,0:T(8,128)S(1)} %get-tuple-element.60.refs_2_, f32[8,4096]{1,0:T(8,128)S(1)} %collective-permute-done.6.refs_3_, ...), custom_call_target="tpu_custom_call" | custom-call | flops 1073741824 | bytes 8388608 | tf_op jit(solution)/shard_map/forward/pallas_call | solution.py:206
  27.3 1.2 %forward.7 = (f32[8,4096]{1,0:T(8,128)S(1)}, f32[2,8,1024]{2,1,0:T(8,128)S(1)}, f32[2,8,512]{2,1,0:T(8,128)S(1)}) custom-call(f32[8,4096]{1,0:T(8,128)S(1)} %get-tuple-element.56.refs_1_.refs_0_.refs_2_, f32[8,4096]{1,0:T(8,128)S(1)} %get-tuple-element.56.refs_1_.refs_0_.refs_2_, f32[8,4096]{1,0:T(8,128)S(1)} %backward.10.refs_2_, ...), custom_call_target="tpu_custom_call" | custom-call | flops 1073741824 | bytes 8388608 | tf_op jit(solution)/shard_map/forward/pallas_call | solution.py:206
  28.5 1.5 %collective-permute-start.10 = (f32[2,8,512]{2,1,0:T(8,128)S(1)}, f32[2,8,512]{2,1,0:T(8,128)S(1)}, u32[]{:S(2)}, u32[]{:S(2)}) collective-permute-start(f32[2,8,512]{2,1,0:T(8,128)S(1)} %get-tuple-element.66), channel_id=1, source_target_pairs={{0,6},{2,4},{4,2},{6,0},{8,14},{10,12},{12,10},{14,8},{1,7},{3,5},... | collective-permute-start | bytes 98312 | tf_op jit(solution)/shard_map/ppermute | solution.py:495
  30.1 1.8 %collective-permute-start.8 = (f32[2,8,512]{2,1,0:T(8,128)S(1)}, f32[2,8,512]{2,1,0:T(8,128)S(1)}, u32[]{:S(2)}, u32[]{:S(2)}) collective-permute-start(f32[2,8,512]{2,1,0:T(8,128)S(1)} %get-tuple-element.66), channel_id=1, source_target_pairs={{0,2},{2,0},{4,6},{6,4},{8,10},{10,8},{12,14},{14,12},{1,3},{3,1},... | collective-permute-start | bytes 98312 | tf_op jit(solution)/shard_map/ppermute | solution.py:495
  32.0 1.9 %collective-permute-start.13 = (f32[2,8,1024]{2,1,0:T(8,128)S(1)}, f32[2,8,1024]{2,1,0:T(8,128)S(1)}, u32[]{:S(2)}, u32[]{:S(2)}) collective-permute-start(f32[2,8,1024]{2,1,0:T(8,128)S(1)} %get-tuple-element.70), channel_id=1, source_target_pairs={{0,3},{2,5},{4,7},{6,9},{8,11},{10,13},{12,15},{3,0},{5,2},{7,4},{... | collective-permute-start | bytes 196616 | tf_op jit(solution)/shard_map/ppermute | solution.py:491
  34.1 3.0 %collective-permute-start.11 = (f32[2,8,512]{2,1,0:T(8,128)S(1)}, f32[2,8,512]{2,1,0:T(8,128)S(1)}, u32[]{:S(2)}, u32[]{:S(2)}) collective-permute-start(f32[2,8,512]{2,1,0:T(8,128)S(1)} %add_add_fusion.2.here_ref), channel_id=1, source_target_pairs={{0,8},{2,10},{4,12},{6,14},{8,0},{10,2},{12,4},{14,6},{1,9},{3,11}... | collective-permute-start | bytes 98312 | tf_op jit(solution)/shard_map/ppermute | solution.py:495
  37.0 2.2 %collective-permute-done.11.there_ref = f32[2,8,512]{2,1,0:T(8,128)S(1)} collective-permute-done((f32[2,8,512]{2,1,0:T(8,128)S(1)}, f32[2,8,512]{2,1,0:T(8,128)S(1)}, u32[]{:S(2)}, u32[]{:S(2)}) %collective-permute-start.11) | collective-permute-done | bytes 32800 | tf_op jit(solution)/shard_map/ppermute | solution.py:495
  40.5 1.3 %backward.11 = (f32[8,4096]{1,0:T(8,128)S(1)}, bf16[16,512]{1,0:T(8,128)(2,1)S(1)}) custom-call(f32[2,8,512]{2,1,0:T(8,128)S(1)} %get-tuple-element.67.resid_ref, f32[2,8,128]{2,1,0:T(8,128)S(1)} %get-tuple-element.68.own_ref, f32[2,8,128]{2,1,0:T(8,128)S(1)} %collective-permute-done.12.other_ref, f32[2,512]{1,0:T(2,128)S(1)} %copy-done.2, ...), custom_call_target="tpu_custom_call" | custom-call | flops 1073741824 | bytes 8388608 | tf_op jit(solution)/shard_map/backward/pallas_call | solution.py:408
  42.1 1.2 %backward.12.refs_2_ = f32[8,4096]{1,0:T(8,128)S(1)} custom-call(bf16[16,512]{1,0:T(8,128)(2,1)S(1)} %get-tuple-element.74.rows_ref, f32[8,4096]{1,0:T(8,128)S(1)} %get-tuple-element.75.couple_ref, bf16[2,2,512,4096]{3,2,1,0:T(8,128)(2,1)S(1)} %get-tuple-element.59.split_ref), custom_call_target="tpu_custom_call" | custom-call | flops 1073741824 | bytes 8388608 | tf_op jit(solution)/shard_map/backward/pallas_call | solution.py:421
  43.6 1.2 %forward.8 = (f32[8,4096]{1,0:T(8,128)S(1)}, f32[8,512]{1,0:T(8,128)S(1)}) custom-call(f32[8,4096]{1,0:T(8,128)S(1)} %get-tuple-element.62.refs_5_.refs_0_, f32[8,4096]{1,0:T(8,128)S(1)} %get-tuple-element.51.refs_0_.refs_1_.prior_ref, f32[8,4096]{1,0:T(8,128)S(1)} %get-tuple-element.72.refs_2_, f32[8,4096]{1,0:T(8,128)S(1)} %collective-permute-done.14.refs_3_, ...), custom_call_target="tpu_custom_call" | custom-call | flops 1073741824 | bytes 8388608 | tf_op jit(solution)/shard_map/forward/pallas_call | solution.py:206
  44.8 1.2 %forward.9 = (f32[8,4096]{1,0:T(8,128)S(1)}, f32[2,8,1024]{2,1,0:T(8,128)S(1)}, f32[2,8,512]{2,1,0:T(8,128)S(1)}) custom-call(f32[8,4096]{1,0:T(8,128)S(1)} %get-tuple-element.69.refs_1_.refs_0_, f32[8,4096]{1,0:T(8,128)S(1)} %get-tuple-element.56.refs_1_.refs_0_.refs_2_, f32[8,4096]{1,0:T(8,128)S(1)} %backward.12.refs_2_, ...), custom_call_target="tpu_custom_call" | custom-call | flops 1073741824 | bytes 8388608 | tf_op jit(solution)/shard_map/forward/pallas_call | solution.py:206
  46.0 2.7 %collective-permute-start.18 = (f32[2,8,512]{2,1,0:T(8,128)S(1)}, f32[2,8,512]{2,1,0:T(8,128)S(1)}, u32[]{:S(2)}, u32[]{:S(2)}) collective-permute-start(f32[2,8,512]{2,1,0:T(8,128)S(1)} %get-tuple-element.77), channel_id=1, source_target_pairs={{0,6},{2,4},{4,2},{6,0},{8,14},{10,12},{12,10},{14,8},{1,7},{3,5},... | collective-permute-start | bytes 98312 | tf_op jit(solution)/shard_map/ppermute | solution.py:495
  49.5 2.4 %collective-permute-start.21 = (f32[2,8,1024]{2,1,0:T(8,128)S(1)}, f32[2,8,1024]{2,1,0:T(8,128)S(1)}, u32[]{:S(2)}, u32[]{:S(2)}) collective-permute-start(f32[2,8,1024]{2,1,0:T(8,128)S(1)} %get-tuple-element.81), channel_id=1, source_target_pairs={{0,3},{2,5},{4,7},{6,9},{8,11},{10,13},{12,15},{3,0},{5,2},{7,4},{... | collective-permute-start | bytes 196616 | tf_op jit(solution)/shard_map/ppermute | solution.py:491
  53.0 2.9 %collective-permute-start.19 = (f32[2,8,512]{2,1,0:T(8,128)S(1)}, f32[2,8,512]{2,1,0:T(8,128)S(1)}, u32[]{:S(2)}, u32[]{:S(2)}) collective-permute-start(f32[2,8,512]{2,1,0:T(8,128)S(1)} %add_add_fusion.1.here_ref), channel_id=1, source_target_pairs={{0,8},{2,10},{4,12},{6,14},{8,0},{10,2},{12,4},{14,6},{1,9},{3,11}... | collective-permute-start | bytes 98312 | tf_op jit(solution)/shard_map/ppermute | solution.py:495
  55.9 2.0 %collective-permute-done.19.there_ref = f32[2,8,512]{2,1,0:T(8,128)S(1)} collective-permute-done((f32[2,8,512]{2,1,0:T(8,128)S(1)}, f32[2,8,512]{2,1,0:T(8,128)S(1)}, u32[]{:S(2)}, u32[]{:S(2)}) %collective-permute-start.19) | collective-permute-done | bytes 32800 | tf_op jit(solution)/shard_map/ppermute | solution.py:495
  59.2 1.3 %backward.13 = (f32[8,4096]{1,0:T(8,128)S(1)}, bf16[16,512]{1,0:T(8,128)(2,1)S(1)}) custom-call(f32[2,8,512]{2,1,0:T(8,128)S(1)} %get-tuple-element.78.resid_ref, f32[2,8,128]{2,1,0:T(8,128)S(1)} %get-tuple-element.79.own_ref, f32[2,8,128]{2,1,0:T(8,128)S(1)} %collective-permute-done.20.other_ref, f32[2,512]{1,0:T(2,128)S(1)} %copy-done.2, ...), custom_call_target="tpu_custom_call" | custom-call | flops 1073741824 | bytes 8388608 | tf_op jit(solution)/shard_map/backward/pallas_call | solution.py:408
  60.7 1.2 %backward.14.refs_2_ = f32[8,4096]{1,0:T(8,128)S(1)} custom-call(bf16[16,512]{1,0:T(8,128)(2,1)S(1)} %get-tuple-element.85.rows_ref, f32[8,4096]{1,0:T(8,128)S(1)} %get-tuple-element.86.couple_ref, bf16[2,2,512,4096]{3,2,1,0:T(8,128)(2,1)S(1)} %get-tuple-element.59.split_ref), custom_call_target="tpu_custom_call" | custom-call | flops 1073741824 | bytes 8388608 | tf_op jit(solution)/shard_map/backward/pallas_call | solution.py:421
  62.3 1.2 %forward.10 = (f32[8,4096]{1,0:T(8,128)S(1)}, f32[8,512]{1,0:T(8,128)S(1)}) custom-call(f32[8,4096]{1,0:T(8,128)S(1)} %get-tuple-element.73.refs_5_.refs_0_, f32[8,4096]{1,0:T(8,128)S(1)} %get-tuple-element.51.refs_0_.refs_1_.prior_ref, f32[8,4096]{1,0:T(8,128)S(1)} %get-tuple-element.83.refs_2_, f32[8,4096]{1,0:T(8,128)S(1)} %collective-permute-done.22.refs_3_, ...), custom_call_target="tpu_custom_call" | custom-call | flops 1073741824 | bytes 8388608 | tf_op jit(solution)/shard_map/forward/pallas_call | solution.py:206
  63.5 1.2 %forward.11 = (f32[8,4096]{1,0:T(8,128)S(1)}, f32[2,8,1024]{2,1,0:T(8,128)S(1)}, f32[2,8,512]{2,1,0:T(8,128)S(1)}) custom-call(f32[8,4096]{1,0:T(8,128)S(1)} %get-tuple-element.80.refs_1_.refs_0_, f32[8,4096]{1,0:T(8,128)S(1)} %get-tuple-element.56.refs_1_.refs_0_.refs_2_, f32[8,4096]{1,0:T(8,128)S(1)} %backward.14.refs_2_, ...), custom_call_target="tpu_custom_call" | custom-call | flops 1073741824 | bytes 8388608 | tf_op jit(solution)/shard_map/forward/pallas_call | solution.py:206
  64.6 1.9 %collective-permute-start.26 = (f32[2,8,512]{2,1,0:T(8,128)S(1)}, f32[2,8,512]{2,1,0:T(8,128)S(1)}, u32[]{:S(2)}, u32[]{:S(2)}) collective-permute-start(f32[2,8,512]{2,1,0:T(8,128)S(1)} %get-tuple-element.88), channel_id=1, source_target_pairs={{0,6},{2,4},{4,2},{6,0},{8,14},{10,12},{12,10},{14,8},{1,7},{3,5},... | collective-permute-start | bytes 98312 | tf_op jit(solution)/shard_map/ppermute | solution.py:495
  66.6 1.5 %collective-permute-start.24 = (f32[2,8,512]{2,1,0:T(8,128)S(1)}, f32[2,8,512]{2,1,0:T(8,128)S(1)}, u32[]{:S(2)}, u32[]{:S(2)}) collective-permute-start(f32[2,8,512]{2,1,0:T(8,128)S(1)} %get-tuple-element.88), channel_id=1, source_target_pairs={{0,2},{2,0},{4,6},{6,4},{8,10},{10,8},{12,14},{14,12},{1,3},{3,1},... | collective-permute-start | bytes 98312 | tf_op jit(solution)/shard_map/ppermute | solution.py:495
  68.2 1.9 %collective-permute-start.29 = (f32[2,8,1024]{2,1,0:T(8,128)S(1)}, f32[2,8,1024]{2,1,0:T(8,128)S(1)}, u32[]{:S(2)}, u32[]{:S(2)}) collective-permute-start(f32[2,8,1024]{2,1,0:T(8,128)S(1)} %get-tuple-element.92), channel_id=1, source_target_pairs={{0,3},{2,5},{4,7},{6,9},{8,11},{10,13},{12,15},{3,0},{5,2},{7,4},{... | collective-permute-start | bytes 196616 | tf_op jit(solution)/shard_map/ppermute | solution.py:491
  70.6 2.9 %collective-permute-start.27 = (f32[2,8,512]{2,1,0:T(8,128)S(1)}, f32[2,8,512]{2,1,0:T(8,128)S(1)}, u32[]{:S(2)}, u32[]{:S(2)}) collective-permute-start(f32[2,8,512]{2,1,0:T(8,128)S(1)} %add_add_fusion.here_ref), channel_id=1, source_target_pairs={{0,8},{2,10},{4,12},{6,14},{8,0},{10,2},{12,4},{14,6},{1,9},{3,11}... | collective-permute-start | bytes 98312 | tf_op jit(solution)/shard_map/ppermute | solution.py:495
  73.5 2.3 %collective-permute-done.27.there_ref = f32[2,8,512]{2,1,0:T(8,128)S(1)} collective-permute-done((f32[2,8,512]{2,1,0:T(8,128)S(1)}, f32[2,8,512]{2,1,0:T(8,128)S(1)}, u32[]{:S(2)}, u32[]{:S(2)}) %collective-permute-start.27) | collective-permute-done | bytes 32800 | tf_op jit(solution)/shard_map/ppermute | solution.py:495
  77.1 1.3 %backward.15 = (f32[8,4096]{1,0:T(8,128)S(1)}, bf16[16,512]{1,0:T(8,128)(2,1)S(1)}) custom-call(f32[2,8,512]{2,1,0:T(8,128)S(1)} %get-tuple-element.89.resid_ref, f32[2,8,128]{2,1,0:T(8,128)S(1)} %get-tuple-element.90.own_ref, f32[2,8,128]{2,1,0:T(8,128)S(1)} %collective-permute-done.28.other_ref, f32[2,512]{1,0:T(2,128)S(1)} %copy-done.2, ...), custom_call_target="tpu_custom_call" | custom-call | flops 1073741824 | bytes 8388608 | tf_op jit(solution)/shard_map/backward/pallas_call | solution.py:408
  (72 shorter events, 15.6 us)
Async XLA Ops:
  8.3 7.0 %collective-permute-start.2 = (f32[2,8,512]{2,1,0:T(8,128)S(1)}, f32[2,8,512]{2,1,0:T(8,128)S(1)}, u32[]{:S(2)}, u32[]{:S(2)}) collective-permute-start(f32[2,8,512]{2,1,0:T(8,128)S(1)} %get-tuple-element.52), channel_id=1, source_target_pairs={{0,6},{2,4},{4,2},{6,0},{8,14},{10,12},{12,10},{14,8},{1,7},{3,5},... | collective-permute-start | bytes 98312 | tf_op jit(solution)/shard_map/ppermute | solution.py:495
  12.4 3.9 %collective-permute-start.1 = (f32[2,8,512]{2,1,0:T(8,128)S(1)}, f32[2,8,512]{2,1,0:T(8,128)S(1)}, u32[]{:S(2)}, u32[]{:S(2)}) collective-permute-start(f32[2,8,512]{2,1,0:T(8,128)S(1)} %get-tuple-element.52), channel_id=1, source_target_pairs={{0,4},{2,6},{4,0},{6,2},{8,12},{10,14},{12,8},{14,10},{1,5},{3,7},... | collective-permute-start | bytes 98312 | tf_op jit(solution)/shard_map/ppermute | solution.py:495
  12.8 3.9 %collective-permute-start = (f32[2,8,512]{2,1,0:T(8,128)S(1)}, f32[2,8,512]{2,1,0:T(8,128)S(1)}, u32[]{:S(2)}, u32[]{:S(2)}) collective-permute-start(f32[2,8,512]{2,1,0:T(8,128)S(1)} %get-tuple-element.52), channel_id=1, source_target_pairs={{0,2},{2,0},{4,6},{6,4},{8,10},{10,8},{12,14},{14,12},{1,3},{3,1},... | collective-permute-start | bytes 98312 | tf_op jit(solution)/shard_map/ppermute | solution.py:495
  13.0 8.8 %collective-permute-start.5 = (f32[2,8,1024]{2,1,0:T(8,128)S(1)}, f32[2,8,1024]{2,1,0:T(8,128)S(1)}, u32[]{:S(2)}, u32[]{:S(2)}) collective-permute-start(f32[2,8,1024]{2,1,0:T(8,128)S(1)} %get-tuple-element.57), channel_id=1, source_target_pairs={{0,3},{2,5},{4,7},{6,9},{8,11},{10,13},{12,15},{3,0},{5,2},{7,4},{... | collective-permute-start | bytes 196616 | tf_op jit(solution)/shard_map/ppermute | solution.py:491
  16.8 4.9 %collective-permute-start.3 = (f32[2,8,512]{2,1,0:T(8,128)S(1)}, f32[2,8,512]{2,1,0:T(8,128)S(1)}, u32[]{:S(2)}, u32[]{:S(2)}) collective-permute-start(f32[2,8,512]{2,1,0:T(8,128)S(1)} %add_add_fusion.3.here_ref), channel_id=1, source_target_pairs={{0,8},{2,10},{4,12},{6,14},{8,0},{10,2},{12,4},{14,6},{1,9},{3,11}... | collective-permute-start | bytes 98312 | tf_op jit(solution)/shard_map/ppermute | solution.py:495
  21.8 1.2 %collective-permute-start.4 = (f32[2,8,128]{2,1,0:T(8,128)S(1)}, f32[2,8,128]{2,1,0:T(8,128)S(1)}, u32[]{:S(2)}, u32[]{:S(2)}) collective-permute-start(f32[2,8,128]{2,1,0:T(8,128)S(1)} %get-tuple-element.55.own_ref), channel_id=1, source_target_pairs={{0,1},{1,0},{2,3},{3,2},{4,5},{5,4},{6,7},{7,6},{8,9},{9,8},{10,11... | collective-permute-start | bytes 24584 | tf_op jit(solution)/shard_map/ppermute | solution.py:484
  24.3 1.7 %collective-permute-start.6 = (f32[8,4096]{1,0:T(8,128)S(1)}, f32[8,4096]{1,0:T(8,128)S(1)}, u32[]{:S(2)}, u32[]{:S(2)}) collective-permute-start(f32[8,4096]{1,0:T(8,128)S(1)} %get-tuple-element.60.refs_2_), channel_id=1, source_target_pairs={{0,1},{1,0},{2,3},{3,2},{4,5},{5,4},{6,7},{7,6},{8,9},{9,8},{10,11... | collective-permute-start | bytes 393224 | tf_op jit(solution)/shard_map/ppermute | solution.py:484
  25.7 1.5 %collective-permute-start.7 = (f32[8,4096]{1,0:T(8,128)S(1)}, f32[8,4096]{1,0:T(8,128)S(1)}, u32[]{:S(2)}, u32[]{:S(2)}) collective-permute-start(f32[8,4096]{1,0:T(8,128)S(1)} %backward.10.refs_2_), channel_id=1, source_target_pairs={{0,1},{1,0},{2,3},{3,2},{4,5},{5,4},{6,7},{7,6},{8,9},{9,8},{10,11... | collective-permute-start | bytes 393224 | tf_op jit(solution)/shard_map/ppermute | solution.py:484
  28.5 5.4 %collective-permute-start.10 = (f32[2,8,512]{2,1,0:T(8,128)S(1)}, f32[2,8,512]{2,1,0:T(8,128)S(1)}, u32[]{:S(2)}, u32[]{:S(2)}) collective-permute-start(f32[2,8,512]{2,1,0:T(8,128)S(1)} %get-tuple-element.66), channel_id=1, source_target_pairs={{0,6},{2,4},{4,2},{6,0},{8,14},{10,12},{12,10},{14,8},{1,7},{3,5},... | collective-permute-start | bytes 98312 | tf_op jit(solution)/shard_map/ppermute | solution.py:495
  30.0 3.9 %collective-permute-start.9 = (f32[2,8,512]{2,1,0:T(8,128)S(1)}, f32[2,8,512]{2,1,0:T(8,128)S(1)}, u32[]{:S(2)}, u32[]{:S(2)}) collective-permute-start(f32[2,8,512]{2,1,0:T(8,128)S(1)} %get-tuple-element.66), channel_id=1, source_target_pairs={{0,4},{2,6},{4,0},{6,2},{8,12},{10,14},{12,8},{14,10},{1,5},{3,7},... | collective-permute-start | bytes 98312 | tf_op jit(solution)/shard_map/ppermute | solution.py:495
  30.1 3.9 %collective-permute-start.8 = (f32[2,8,512]{2,1,0:T(8,128)S(1)}, f32[2,8,512]{2,1,0:T(8,128)S(1)}, u32[]{:S(2)}, u32[]{:S(2)}) collective-permute-start(f32[2,8,512]{2,1,0:T(8,128)S(1)} %get-tuple-element.66), channel_id=1, source_target_pairs={{0,2},{2,0},{4,6},{6,4},{8,10},{10,8},{12,14},{14,12},{1,3},{3,1},... | collective-permute-start | bytes 98312 | tf_op jit(solution)/shard_map/ppermute | solution.py:495
  32.0 7.5 %collective-permute-start.13 = (f32[2,8,1024]{2,1,0:T(8,128)S(1)}, f32[2,8,1024]{2,1,0:T(8,128)S(1)}, u32[]{:S(2)}, u32[]{:S(2)}) collective-permute-start(f32[2,8,1024]{2,1,0:T(8,128)S(1)} %get-tuple-element.70), channel_id=1, source_target_pairs={{0,3},{2,5},{4,7},{6,9},{8,11},{10,13},{12,15},{3,0},{5,2},{7,4},{... | collective-permute-start | bytes 196616 | tf_op jit(solution)/shard_map/ppermute | solution.py:491
  34.1 5.1 %collective-permute-start.11 = (f32[2,8,512]{2,1,0:T(8,128)S(1)}, f32[2,8,512]{2,1,0:T(8,128)S(1)}, u32[]{:S(2)}, u32[]{:S(2)}) collective-permute-start(f32[2,8,512]{2,1,0:T(8,128)S(1)} %add_add_fusion.2.here_ref), channel_id=1, source_target_pairs={{0,8},{2,10},{4,12},{6,14},{8,0},{10,2},{12,4},{14,6},{1,9},{3,11}... | collective-permute-start | bytes 98312 | tf_op jit(solution)/shard_map/ppermute | solution.py:495
  39.3 1.2 %collective-permute-start.12 = (f32[2,8,128]{2,1,0:T(8,128)S(1)}, f32[2,8,128]{2,1,0:T(8,128)S(1)}, u32[]{:S(2)}, u32[]{:S(2)}) collective-permute-start(f32[2,8,128]{2,1,0:T(8,128)S(1)} %get-tuple-element.68.own_ref), channel_id=1, source_target_pairs={{0,1},{1,0},{2,3},{3,2},{4,5},{5,4},{6,7},{7,6},{8,9},{9,8},{10,11... | collective-permute-start | bytes 24584 | tf_op jit(solution)/shard_map/ppermute | solution.py:484
  41.9 1.7 %collective-permute-start.14 = (f32[8,4096]{1,0:T(8,128)S(1)}, f32[8,4096]{1,0:T(8,128)S(1)}, u32[]{:S(2)}, u32[]{:S(2)}) collective-permute-start(f32[8,4096]{1,0:T(8,128)S(1)} %get-tuple-element.72.refs_2_), channel_id=1, source_target_pairs={{0,1},{1,0},{2,3},{3,2},{4,5},{5,4},{6,7},{7,6},{8,9},{9,8},{10,11... | collective-permute-start | bytes 393224 | tf_op jit(solution)/shard_map/ppermute | solution.py:484
  43.2 1.5 %collective-permute-start.15 = (f32[8,4096]{1,0:T(8,128)S(1)}, f32[8,4096]{1,0:T(8,128)S(1)}, u32[]{:S(2)}, u32[]{:S(2)}) collective-permute-start(f32[8,4096]{1,0:T(8,128)S(1)} %backward.12.refs_2_), channel_id=1, source_target_pairs={{0,1},{1,0},{2,3},{3,2},{4,5},{5,4},{6,7},{7,6},{8,9},{9,8},{10,11... | collective-permute-start | bytes 393224 | tf_op jit(solution)/shard_map/ppermute | solution.py:484
  46.0 5.9 %collective-permute-start.18 = (f32[2,8,512]{2,1,0:T(8,128)S(1)}, f32[2,8,512]{2,1,0:T(8,128)S(1)}, u32[]{:S(2)}, u32[]{:S(2)}) collective-permute-start(f32[2,8,512]{2,1,0:T(8,128)S(1)} %get-tuple-element.77), channel_id=1, source_target_pairs={{0,6},{2,4},{4,2},{6,0},{8,14},{10,12},{12,10},{14,8},{1,7},{3,5},... | collective-permute-start | bytes 98312 | tf_op jit(solution)/shard_map/ppermute | solution.py:495
  48.7 3.9 %collective-permute-start.17 = (f32[2,8,512]{2,1,0:T(8,128)S(1)}, f32[2,8,512]{2,1,0:T(8,128)S(1)}, u32[]{:S(2)}, u32[]{:S(2)}) collective-permute-start(f32[2,8,512]{2,1,0:T(8,128)S(1)} %get-tuple-element.77), channel_id=1, source_target_pairs={{0,4},{2,6},{4,0},{6,2},{8,12},{10,14},{12,8},{14,10},{1,5},{3,7},... | collective-permute-start | bytes 98312 | tf_op jit(solution)/shard_map/ppermute | solution.py:495
  49.0 3.9 %collective-permute-start.16 = (f32[2,8,512]{2,1,0:T(8,128)S(1)}, f32[2,8,512]{2,1,0:T(8,128)S(1)}, u32[]{:S(2)}, u32[]{:S(2)}) collective-permute-start(f32[2,8,512]{2,1,0:T(8,128)S(1)} %get-tuple-element.77), channel_id=1, source_target_pairs={{0,2},{2,0},{4,6},{6,4},{8,10},{10,8},{12,14},{14,12},{1,3},{3,1},... | collective-permute-start | bytes 98312 | tf_op jit(solution)/shard_map/ppermute | solution.py:495
  49.5 8.6 %collective-permute-start.21 = (f32[2,8,1024]{2,1,0:T(8,128)S(1)}, f32[2,8,1024]{2,1,0:T(8,128)S(1)}, u32[]{:S(2)}, u32[]{:S(2)}) collective-permute-start(f32[2,8,1024]{2,1,0:T(8,128)S(1)} %get-tuple-element.81), channel_id=1, source_target_pairs={{0,3},{2,5},{4,7},{6,9},{8,11},{10,13},{12,15},{3,0},{5,2},{7,4},{... | collective-permute-start | bytes 196616 | tf_op jit(solution)/shard_map/ppermute | solution.py:491
  53.0 4.9 %collective-permute-start.19 = (f32[2,8,512]{2,1,0:T(8,128)S(1)}, f32[2,8,512]{2,1,0:T(8,128)S(1)}, u32[]{:S(2)}, u32[]{:S(2)}) collective-permute-start(f32[2,8,512]{2,1,0:T(8,128)S(1)} %add_add_fusion.1.here_ref), channel_id=1, source_target_pairs={{0,8},{2,10},{4,12},{6,14},{8,0},{10,2},{12,4},{14,6},{1,9},{3,11}... | collective-permute-start | bytes 98312 | tf_op jit(solution)/shard_map/ppermute | solution.py:495
  58.0 1.2 %collective-permute-start.20 = (f32[2,8,128]{2,1,0:T(8,128)S(1)}, f32[2,8,128]{2,1,0:T(8,128)S(1)}, u32[]{:S(2)}, u32[]{:S(2)}) collective-permute-start(f32[2,8,128]{2,1,0:T(8,128)S(1)} %get-tuple-element.79.own_ref), channel_id=1, source_target_pairs={{0,1},{1,0},{2,3},{3,2},{4,5},{5,4},{6,7},{7,6},{8,9},{9,8},{10,11... | collective-permute-start | bytes 24584 | tf_op jit(solution)/shard_map/ppermute | solution.py:484
  60.5 1.7 %collective-permute-start.22 = (f32[8,4096]{1,0:T(8,128)S(1)}, f32[8,4096]{1,0:T(8,128)S(1)}, u32[]{:S(2)}, u32[]{:S(2)}) collective-permute-start(f32[8,4096]{1,0:T(8,128)S(1)} %get-tuple-element.83.refs_2_), channel_id=1, source_target_pairs={{0,1},{1,0},{2,3},{3,2},{4,5},{5,4},{6,7},{7,6},{8,9},{9,8},{10,11... | collective-permute-start | bytes 393224 | tf_op jit(solution)/shard_map/ppermute | solution.py:484
  61.9 1.5 %collective-permute-start.23 = (f32[8,4096]{1,0:T(8,128)S(1)}, f32[8,4096]{1,0:T(8,128)S(1)}, u32[]{:S(2)}, u32[]{:S(2)}) collective-permute-start(f32[8,4096]{1,0:T(8,128)S(1)} %backward.14.refs_2_), channel_id=1, source_target_pairs={{0,1},{1,0},{2,3},{3,2},{4,5},{5,4},{6,7},{7,6},{8,9},{9,8},{10,11... | collective-permute-start | bytes 393224 | tf_op jit(solution)/shard_map/ppermute | solution.py:484
  64.6 5.4 %collective-permute-start.26 = (f32[2,8,512]{2,1,0:T(8,128)S(1)}, f32[2,8,512]{2,1,0:T(8,128)S(1)}, u32[]{:S(2)}, u32[]{:S(2)}) collective-permute-start(f32[2,8,512]{2,1,0:T(8,128)S(1)} %get-tuple-element.88), channel_id=1, source_target_pairs={{0,6},{2,4},{4,2},{6,0},{8,14},{10,12},{12,10},{14,8},{1,7},{3,5},... | collective-permute-start | bytes 98312 | tf_op jit(solution)/shard_map/ppermute | solution.py:495
  66.6 3.9 %collective-permute-start.25 = (f32[2,8,512]{2,1,0:T(8,128)S(1)}, f32[2,8,512]{2,1,0:T(8,128)S(1)}, u32[]{:S(2)}, u32[]{:S(2)}) collective-permute-start(f32[2,8,512]{2,1,0:T(8,128)S(1)} %get-tuple-element.88), channel_id=1, source_target_pairs={{0,4},{2,6},{4,0},{6,2},{8,12},{10,14},{12,8},{14,10},{1,5},{3,7},... | collective-permute-start | bytes 98312 | tf_op jit(solution)/shard_map/ppermute | solution.py:495
  66.6 3.9 %collective-permute-start.24 = (f32[2,8,512]{2,1,0:T(8,128)S(1)}, f32[2,8,512]{2,1,0:T(8,128)S(1)}, u32[]{:S(2)}, u32[]{:S(2)}) collective-permute-start(f32[2,8,512]{2,1,0:T(8,128)S(1)} %get-tuple-element.88), channel_id=1, source_target_pairs={{0,2},{2,0},{4,6},{6,4},{8,10},{10,8},{12,14},{14,12},{1,3},{3,1},... | collective-permute-start | bytes 98312 | tf_op jit(solution)/shard_map/ppermute | solution.py:495
  68.2 7.9 %collective-permute-start.29 = (f32[2,8,1024]{2,1,0:T(8,128)S(1)}, f32[2,8,1024]{2,1,0:T(8,128)S(1)}, u32[]{:S(2)}, u32[]{:S(2)}) collective-permute-start(f32[2,8,1024]{2,1,0:T(8,128)S(1)} %get-tuple-element.92), channel_id=1, source_target_pairs={{0,3},{2,5},{4,7},{6,9},{8,11},{10,13},{12,15},{3,0},{5,2},{7,4},{... | collective-permute-start | bytes 196616 | tf_op jit(solution)/shard_map/ppermute | solution.py:491
  70.6 5.2 %collective-permute-start.27 = (f32[2,8,512]{2,1,0:T(8,128)S(1)}, f32[2,8,512]{2,1,0:T(8,128)S(1)}, u32[]{:S(2)}, u32[]{:S(2)}) collective-permute-start(f32[2,8,512]{2,1,0:T(8,128)S(1)} %add_add_fusion.here_ref), channel_id=1, source_target_pairs={{0,8},{2,10},{4,12},{6,14},{8,0},{10,2},{12,4},{14,6},{1,9},{3,11}... | collective-permute-start | bytes 98312 | tf_op jit(solution)/shard_map/ppermute | solution.py:495
  78.4 2.0 %collective-permute-start.30 = (f32[8,4096]{1,0:T(8,128)S(1)}, f32[8,4096]{1,0:T(8,128)S(1)}, u32[]{:S(2)}, u32[]{:S(2)}) collective-permute-start(f32[8,4096]{1,0:T(8,128)S(1)} %get-tuple-element.94.own_ref), channel_id=1, source_target_pairs={{0,1},{1,0},{2,3},{3,2},{4,5},{5,4},{6,7},{7,6},{8,9},{9,8},{10,11... | collective-permute-start | bytes 393224 | tf_op jit(solution)/shard_map/ppermute | solution.py:484
  79.9 1.3 %collective-permute-start.31 = (f32[8,2048]{1,0:T(8,128)S(1)}, f32[8,2048]{1,0:T(8,128)S(1)}, u32[]{:S(2)}, u32[]{:S(2)}) collective-permute-start(f32[8,2048]{1,0:T(8,128)S(1)} %backward.16.refs_3_), channel_id=1, source_target_pairs={{0,1},{1,0},{2,3},{3,2},{4,5},{5,4},{6,7},{7,6},{8,9},{9,8},{10,11... | collective-permute-start | bytes 196616 | tf_op jit(solution)/shard_map/ppermute | solution.py:484
  80.3 1.3 %collective-permute-start.32 = (f32[8,2048]{1,0:T(8,128)S(1)}, f32[8,2048]{1,0:T(8,128)S(1)}, u32[]{:S(2)}, u32[]{:S(2)}) collective-permute-start(f32[8,2048]{1,0:T(8,128)S(1)} %backward.17.refs_4_), channel_id=1, source_target_pairs={{0,1},{1,0},{2,3},{3,2},{4,5},{5,4},{6,7},{7,6},{8,9},{9,8},{10,11... | collective-permute-start | bytes 196616 | tf_op jit(solution)/shard_map/ppermute | solution.py:484
  (5 other events, 87.8 us)
